TPU v7x, 256 devices: a whole 4x4x8 slice. The times are simulated.
256 devices in a mesh: grp: 8 (over y_lo, x), ctx: 32 (over z, y_hi, core).
Axes of the slice: x: 4, y: 4 (y_hi: 2, y_lo: 2; y = y_hi * 2 + y_lo), z: 8, core: 2. Of those that a mesh axis runs over, the one named last changes fastest.
Arguments:
- saved_mid: bfloat16 [32768, 1024], P(('grp', 'ctx')), parts along dimension 0, may hold values from -6 to 6
- upstream: bfloat16 [32768, 1024], P(('grp', 'ctx')), parts along dimension 0, may hold values from -6 to 6
- queries: bfloat16 [32768, 512], P(('grp', 'ctx')), parts along dimension 0
- keys_in: bfloat16 [32768, 512], P(('grp', 'ctx')), parts along dimension 0
- values_in: bfloat16 [32768, 512], P(('grp', 'ctx')), parts along dimension 0, may hold values from -6 to 6
- attn_out: bfloat16 [32768, 512], P(('grp', 'ctx')), parts along dimension 0, may hold values from -6 to 6
- log_norm: float32 [32768, 8], P(('grp', 'ctx')), parts along dimension 0, as said below
- out_proj: bfloat16 [512, 1024], replicated, may hold values from -0.1875 to 0.1875
- conv_weight: bfloat16 [31, 1024], replicated, may hold values from -2.5 to 2.5
- gates: float32 [32768, 2], P(('grp', 'ctx')), parts along dimension 0, may hold values from 0.1 to 0.9
- expert_ids: int32 [32768, 2], P(('grp', 'ctx')), parts along dimension 0, may hold values from 0 to 31, as said below
- slots: int32 [32768, 2], P(('grp', 'ctx')), parts along dimension 0, may hold values from 0 to 15, as said below
- w_in: bfloat16 [32, 1024, 2048], P('ctx'), may hold values from -0.1875 to 0.1875
- w_out: bfloat16 [32, 2048, 1024], P('ctx'), may hold values from -0.125 to 0.125
Outputs:
- d_mid: bfloat16 [32768, 1024], P(('grp', 'ctx')), parts along dimension 0
- d_queries: bfloat16 [32768, 512], P(('grp', 'ctx')), parts along dimension 0
- d_keys: bfloat16 [32768, 512], P(('grp', 'ctx')), parts along dimension 0
- d_values: bfloat16 [32768, 512], P(('grp', 'ctx')), parts along dimension 0
- d_conv: float32 [248, 1024], P('grp'), parts along dimension 0
- d_gates: bfloat16 [32768, 2], P(('grp', 'ctx')), parts along dimension 0
There are 8 independent parts, one for each index of `grp`. A program takes and returns all parts, laid end to end along the dimension named above; an argument that names none is the same for every part. Nothing has to cross between parts.
Inputs may be any that keep to these rules, and one draw needn't show every extreme that they name: `expert_ids`: each frame names two different experts; within the frames of one block of 128, an expert is named at most 16 times. `slots`: within the frames of one block of 128, the (expert, slot) pairs are all different. log_norm[t, h] is the log of the sum over all 4096 frames u of exp(64 ** -0.5 queries_h[t] . keys_in_h[u]).
All inputs are finite; a program needn't handle non-finite values.
Results may differ from a plain program's by a relative error of at most 0.03.
Values may be sent and summed in bfloat16 or wider, within the bound.
A program may use at most 128 MiB of HBM per device.

v0:
```python
import jax
import jax.numpy as jnp
from jax import lax
from jax.sharding import PartitionSpec as P


def extended(array, sides, width):
    for axis, dim in sides:
        devices, length = (lax.axis_size(axis), array.shape[dim])
        up = [(i, (i + 1) % devices) for i in range(devices - 1)]
        down = [(j, i) for i, j in up]
        last = lax.slice_in_dim(array, length - width, length, axis=dim)
        leading = lax.slice_in_dim(array, 0, width, axis=dim)
        before = lax.ppermute(last, axis, up)
        after = lax.ppermute(leading, axis, down)
        array = jnp.concatenate([before, array, after], axis=dim)
    return array


def from_behind(value, axis, steps):
    count = lax.axis_size(axis)
    pairs = [(source, (source + steps) % count) for source in range(count)]
    return lax.ppermute(value, axis, pairs)


def attention_terms(
    query_rows, dout_rows, norm_rows, delta_rows, key_rows, value_rows, score_scale
):
    scores = (
        jnp.einsum("qhd,khd->hqk", query_rows, key_rows, preferred_element_type=jnp.float32)
        * score_scale
    )
    softmax_rows = jnp.exp(scores - jnp.transpose(norm_rows)[:, :, None])
    dprobs = jnp.einsum("qhd,khd->hqk", dout_rows, value_rows, preferred_element_type=jnp.float32)
    dscores = (softmax_rows * (dprobs - jnp.transpose(delta_rows)[:, :, None])).astype(jnp.bfloat16)
    return (softmax_rows.astype(jnp.bfloat16), dscores)


def query_term(dscores, key_rows, score_scale):
    return (
        jnp.einsum("hqk,khd->qhd", dscores, key_rows, preferred_element_type=jnp.float32)
        * score_scale
    )


def key_terms(softmax_low, dscores, query_rows, dout_rows, score_scale):
    key_grad = (
        jnp.einsum("hqk,qhd->khd", dscores, query_rows, preferred_element_type=jnp.float32)
        * score_scale
    )
    value_grad = jnp.einsum(
        "hqk,qhd->khd", softmax_low, dout_rows, preferred_element_type=jnp.float32
    )
    return (key_grad, value_grad)


def cycle_turn(query_rows, dout_rows, norm_rows, delta_rows, carried, score_scale):
    key_rows, value_rows, key_acc, value_acc, query_acc = carried
    softmax_low, dscores = attention_terms(
        query_rows, dout_rows, norm_rows, delta_rows, key_rows, value_rows, score_scale
    )
    key_grad, value_grad = key_terms(softmax_low, dscores, query_rows, dout_rows, score_scale)
    query_acc = query_acc + query_term(dscores, key_rows, score_scale)
    return (key_rows, value_rows, key_acc + key_grad, value_acc + value_grad, query_acc)


def on_device(
    saved_mid,
    upstream,
    queries,
    keys_in,
    values_in,
    attn_out,
    log_norm,
    out_proj,
    conv_weight,
    gates,
    expert_ids,
    slots,
    w_in,
    w_out,
):
    frames = saved_mid.shape[0]
    model_width = saved_mid.shape[1]
    groups = lax.axis_size("ctx")
    capacity = 4 * frames // groups
    tap_count = conv_weight.shape[0]
    half_taps = (tap_count - 1) // 2
    weights = conv_weight.astype(jnp.float32)
    mid_wide = extended(saved_mid, (("ctx", 0),), half_taps).astype(jnp.float32)
    conv_total = jnp.zeros((frames, model_width), jnp.float32)
    for offset in range(tap_count):
        conv_total = conv_total + weights[offset] * mid_wide[offset : offset + frames]
    mixed_rows = (saved_mid.astype(jnp.float32) + conv_total).astype(jnp.bfloat16)
    flat_index = expert_ids * capacity + slots
    owner_row = (
        jnp.full((groups * capacity,), frames, jnp.int32)
        .at[flat_index.reshape(-1)]
        .set(jnp.repeat(jnp.arange(frames, dtype=jnp.int32), 2))
    )
    blank = jnp.zeros((1, model_width), jnp.bfloat16)
    send_rows = jnp.concatenate([mixed_rows, blank], 0)[owner_row].reshape(
        groups, capacity, model_width
    )
    send_grads = jnp.concatenate([upstream, blank], 0)[owner_row].reshape(
        groups, capacity, model_width
    )
    w_input = w_in[0]
    w_output = w_out[0]
    rows_x = lax.all_to_all(send_rows, "ctx", split_axis=0, concat_axis=0, tiled=True)
    rows_g = lax.all_to_all(send_grads, "ctx", split_axis=0, concat_axis=0, tiled=True)
    senders = rows_x.shape[0]
    slot_count = rows_x.shape[1]
    inputs = rows_x.reshape(senders * slot_count, model_width)
    grads = rows_g.reshape(senders * slot_count, model_width)
    hidden = jnp.dot(inputs, w_input, preferred_element_type=jnp.float32)
    upward = lax.dot_general(
        grads, w_output, (((1,), (1,)), ((), ())), preferred_element_type=jnp.float32
    )
    logistic = jax.nn.sigmoid(hidden)
    gate_unit = jnp.sum(hidden * logistic * upward, axis=1).astype(jnp.bfloat16)
    hidden_grad = (upward * logistic * (1.0 + hidden * (1.0 - logistic))).astype(jnp.bfloat16)
    input_grad = lax.dot_general(
        hidden_grad, w_input, (((1,), (1,)), ((), ())), preferred_element_type=jnp.float32
    ).astype(jnp.bfloat16)
    returned_rows = lax.all_to_all(
        input_grad.reshape(senders, slot_count, model_width),
        "ctx",
        split_axis=0,
        concat_axis=0,
        tiled=True,
    )
    returned_gates = lax.all_to_all(
        gate_unit.reshape(senders, slot_count), "ctx", split_axis=0, concat_axis=0, tiled=True
    )
    picked = returned_rows.reshape(groups * capacity, model_width)[flat_index]
    d_gates = returned_gates.reshape(groups * capacity)[flat_index]
    grad_sum = upstream.astype(jnp.float32) + gates[:, 0:1] * picked[:, 0].astype(jnp.float32)
    grad_sum = grad_sum + gates[:, 1:2] * picked[:, 1].astype(jnp.float32)
    grad_mixed = lax.optimization_barrier(grad_sum.astype(jnp.bfloat16))
    grad_float = grad_mixed.astype(jnp.float32)
    grad_wide = extended(grad_mixed, (("ctx", 0),), half_taps).astype(jnp.float32)
    dmid_total = grad_float
    for offset in range(tap_count):
        first_row = 2 * half_taps - offset
        dmid_total = dmid_total + weights[offset] * grad_wide[first_row : first_row + frames]
    d_mid = dmid_total.astype(jnp.bfloat16)
    local_terms = jnp.stack(
        [
            jnp.sum(mid_wide[offset : offset + frames] * grad_float, axis=0)
            for offset in range(tap_count)
        ]
    )
    d_conv = lax.psum(local_terms.astype(jnp.bfloat16), "ctx").astype(jnp.float32)
    d_out = lax.dot_general(
        d_mid, out_proj, (((1,), (1,)), ((), ())), preferred_element_type=jnp.float32
    )
    d_out = lax.optimization_barrier(d_out.astype(jnp.bfloat16))
    head_count = log_norm.shape[1]
    head_dim = queries.shape[1] // head_count
    score_scale = head_dim ** (-0.5)
    query_heads = queries.reshape(frames, head_count, head_dim)
    key_heads = keys_in.reshape(frames, head_count, head_dim)
    value_heads = values_in.reshape(frames, head_count, head_dim)
    dout_heads = d_out.reshape(frames, head_count, head_dim)
    row_delta = jnp.sum(
        d_out.astype(jnp.float32).reshape(frames, head_count, head_dim)
        * attn_out.astype(jnp.float32).reshape(frames, head_count, head_dim),
        axis=2,
    )
    empty_acc = jnp.zeros((frames, head_count, head_dim), jnp.float32)

    def carry_turn(offset, carried):
        updated = cycle_turn(query_heads, dout_heads, log_norm, row_delta, carried, score_scale)
        key_rows, value_rows = from_behind((updated[0], updated[1]), "ctx", 1)
        key_acc, value_acc = (
            from_behind(updated[2].astype(jnp.bfloat16), "ctx", 1).astype(jnp.float32),
            from_behind(updated[3].astype(jnp.bfloat16), "ctx", 1).astype(jnp.float32),
        )
        return (key_rows, value_rows, key_acc, value_acc, updated[4])

    finished = lax.fori_loop(
        0, groups, carry_turn, (key_heads, value_heads, empty_acc, empty_acc, empty_acc)
    )
    query_grad, key_grad, value_grad = (finished[4], finished[2], finished[3])
    total_width = head_count * head_dim
    d_queries = query_grad.reshape(frames, total_width).astype(jnp.bfloat16)
    d_keys = key_grad.reshape(frames, total_width).astype(jnp.bfloat16)
    d_values = value_grad.reshape(frames, total_width).astype(jnp.bfloat16)
    return (d_mid, d_queries, d_keys, d_values, d_conv, d_gates)


def solution(mesh):
    in_specs = (
        P(("grp", "ctx"), None),
        P(("grp", "ctx"), None),
        P(("grp", "ctx"), None),
        P(("grp", "ctx"), None),
        P(("grp", "ctx"), None),
        P(("grp", "ctx"), None),
        P(("grp", "ctx"), None),
        P(),
        P(),
        P(("grp", "ctx"), None),
        P(("grp", "ctx"), None),
        P(("grp", "ctx"), None),
        P("ctx", None, None),
        P("ctx", None, None),
    )
    out_specs = (
        P(("grp", "ctx"), None),
        P(("grp", "ctx"), None),
        P(("grp", "ctx"), None),
        P(("grp", "ctx"), None),
        P("grp", None),
        P(("grp", "ctx"), None),
    )
    return jax.shard_map(
        on_device, mesh=mesh, in_specs=in_specs, out_specs=out_specs, check_vma=False
    )
```

profile of v0, /device:TPU:6, one launch (start us, length us, event | category | flops | bytes accessed | tf_op | source)
XLA Modules:
  0.0 721.8 jit_solution(4529796055174091933)
XLA Ops:
  11.2 3.0 add_convert_fusion
  14.6 2.8 gather_fusion.1
  17.4 15.5 %all-to-all-start.1 = ((bf16[32,16,1024]{2,1,0:T(8,128)(2,1)}), bf16[32,16,1024]{2,1,0:T(8,128)(2,1)S(1)}, u32[]{:S(2)}, u32[]{:S(2)}) async-start(bf16[32,16,1024]{2,1,0:T(8,128)(2,1)} %bitcast.36), calls=%async_computation.1 | async-start | bytes 2097152 | tf_op jit(solution)/shard_map/all_to_all | solution.py:110
  33.0 2.8 gather_fusion
  35.8 26.3 %all-to-all-done.1 = bf16[32,16,1024]{2,1,0:T(8,128)(2,1)S(1)} async-done(((bf16[32,16,1024]{2,1,0:T(8,128)(2,1)}), bf16[32,16,1024]{2,1,0:T(8,128)(2,1)S(1)}, u32[]{:S(2)}, u32[]{:S(2)}) %all-to-all-start.1) | async-done | bytes 1048608 | tf_op jit(solution)/shard_map/all_to_all | solution.py:110
  62.0 4.9 all-to-all-start
  67.0 6.5 fusion.14
  73.4 22.6 %all-to-all-done = bf16[32,16,1024]{2,1,0:T(8,128)(2,1)} async-done(((bf16[32,16,1024]{2,1,0:T(8,128)(2,1)}), bf16[32,16,1024]{2,1,0:T(8,128)(2,1)}, u32[]{:S(2)}, u32[]{:S(2)}) %all-to-all-start) | async-done | bytes 1048608 | tf_op jit(solution)/shard_map/all_to_all | solution.py:111
  96.1 8.3 %multiply_reduce_fusion = (bf16[512]{0:T(512)(128)(2,1)S(1)}, f32[512,2048]{1,0:T(8,128)}) fusion(f32[512,2048]{1,0:T(8,128)} %fusion.14, bf16[512,1024]{1,0:T(8,128)(2,1)} %bitcast.3, bf16[1,2048,1024]{2,1,0:T(8,128)(2,1)} %param.29), kind=kOutput, calls=%fused_computation.60 | convolution fusion | flops 2153774592 | bytes 13632512 | tf_op jit(solution)/shard_map/dot_general | solution.py:117
  105.0 5.0 all-to-all-start.3
  110.1 9.3 %fusion.18 = bf16[512,1024]{1,0:T(8,128)(2,1)} fusion(bf16[1,1024,2048]{2,1,0:T(8,128)(2,1)} %param.28, f32[512,2048]{1,0:T(8,128)} %fusion.14, f32[512,2048]{1,0:T(8,128)} %get-tuple-element.211), kind=kOutput, calls=%fused_computation.63 | convolution fusion | flops 2157445120 | bytes 13631488 | tf_op jit(solution)/shard_map/dot_general | solution.py:123
  119.5 9.4 %all-to-all-start.2 = ((bf16[32,16,1024]{2,1,0:T(8,128)(2,1)}), bf16[32,16,1024]{2,1,0:T(8,128)(2,1)S(1)}, u32[]{:S(2)}, u32[]{:S(2)}) async-start(bf16[32,16,1024]{2,1,0:T(8,128)(2,1)} %bitcast.136), calls=%async_computation.2 | async-start | bytes 2097152 | tf_op jit(solution)/shard_map/all_to_all | solution.py:126
  138.9 19.1 %all-to-all-done.2 = bf16[32,16,1024]{2,1,0:T(8,128)(2,1)S(1)} async-done(((bf16[32,16,1024]{2,1,0:T(8,128)(2,1)}), bf16[32,16,1024]{2,1,0:T(8,128)(2,1)S(1)}, u32[]{:S(2)}, u32[]{:S(2)}) %all-to-all-start.2) | async-done | bytes 1048608 | tf_op jit(solution)/shard_map/all_to_all | solution.py:126
  168.7 133.2 %psum.7 = bf16[31,1024]{1,0:T(8,128)(2,1)S(1)} all-reduce(bf16[31,1024]{1,0:T(8,128)(2,1)S(1)} %stack.159), channel_id=1, replica_groups=mesh['grp'=8,'ctx'=32] {'ctx'}, use_global_device_ids=true, to_apply=%region_35.0 | all-reduce | flops 31744 | bytes 126976 | tf_op jit(solution)/shard_map/psum | solution.py:154
  306.7 412.7 %while.19 = (s32[]{:T(128)}, bf16[128,8,64]{0,2,1:T(8,128)(2,1)S(1)}, bf16[128,8,64]{0,2,1:T(8,128)(2,1)}, f32[128,8,64]{0,2,1:T(8,128)S(1)}, f32[128,8,64]{0,2,...) while((s32[]{:T(128)}, ...), condition=%wide.region_3.0_spmd.clone, body=%wide.region_2.0_spmd.clone.sunk | while | flops 85458944 | bytes 8003873 | solution.py:182
  310.5 7.2 collective-permute-done.2
  322.8 7.2 collective-permute-done.2
  335.2 7.2 collective-permute-done.2
  347.6 7.2 collective-permute-done.2
  362.0 5.1 collective-permute-done.2
  372.3 4.7 collective-permute-start.3
  382.0 2.8 collective-permute-start.1
  387.7 4.8 collective-permute-start.3
  397.0 3.2 collective-permute-start.1
  405.2 4.8 collective-permute-done.2
  415.0 2.3 collective-permute-start.3
  417.5 4.8 collective-permute-done.2
  429.9 4.8 collective-permute-done.2
  439.8 2.2 collective-permute-start.3
  442.3 4.8 collective-permute-done.2
  454.7 4.8 collective-permute-done.2
  467.0 4.8 collective-permute-done.2
  476.9 2.3 collective-permute-start.3
  479.4 4.8 collective-permute-done.2
  489.4 4.8 collective-permute-start.3
  499.1 2.8 collective-permute-start.1
  504.3 2.3 collective-permute-start.3
  506.8 4.8 collective-permute-done.2
  519.2 4.8 collective-permute-done.2
  529.0 2.2 collective-permute-start.3
  531.6 4.8 collective-permute-done.2
  543.9 4.8 collective-permute-done.2
  556.3 4.8 collective-permute-done.2
  566.1 2.3 collective-permute-start.3
  568.7 4.8 collective-permute-done.2
  578.7 4.7 collective-permute-start.3
  588.3 2.8 collective-permute-start.1
  594.1 4.8 collective-permute-start.3
  603.4 3.2 collective-permute-start.1
  609.0 2.3 collective-permute-start.3
  611.5 4.8 collective-permute-done.2
  621.3 2.3 collective-permute-start.3
  623.9 4.8 collective-permute-done.2
  636.3 4.8 collective-permute-done.2
  646.1 2.2 collective-permute-start.3
  648.6 4.8 collective-permute-done.2
  661.0 4.8 collective-permute-done.2
  673.4 4.8 collective-permute-done.2
  683.2 2.3 collective-permute-start.3
  685.8 4.8 collective-permute-done.2
  695.7 4.8 collective-permute-start.3
  705.4 2.8 collective-permute-start.1
  710.6 2.3 collective-permute-start.3
  713.1 4.8 collective-permute-done.2
  (732 shorter events, 242.9 us)
Async XLA Ops:
  17.4 44.6 %all-to-all-start.1 = ((bf16[32,16,1024]{2,1,0:T(8,128)(2,1)}), bf16[32,16,1024]{2,1,0:T(8,128)(2,1)S(1)}, u32[]{:S(2)}, u32[]{:S(2)}) async-start(bf16[32,16,1024]{2,1,0:T(8,128)(2,1)} %bitcast.36), calls=%async_computation.1 | async-start | bytes 2097152 | tf_op jit(solution)/shard_map/all_to_all | solution.py:110
  62.0 34.0 %all-to-all-start = ((bf16[32,16,1024]{2,1,0:T(8,128)(2,1)}), bf16[32,16,1024]{2,1,0:T(8,128)(2,1)}, u32[]{:S(2)}, u32[]{:S(2)}) async-start(bf16[32,16,1024]{2,1,0:T(8,128)(2,1)} %bitcast.2), calls=%async_computation | async-start | bytes 2097152 | tf_op jit(solution)/shard_map/all_to_all | solution.py:111
  105.0 14.5 %all-to-all-start.3 = ((bf16[32,1,16]{2,1,0:T(2,128)(2,1)}), bf16[32,1,16]{2,1,0:T(2,128)(2,1)S(1)}, u32[]{:S(2)}, u32[]{:S(2)}) async-start(bf16[32,1,16]{2,1,0:T(2,128)(2,1)} %convert_element_type.143), calls=%async_computation.3 | async-start | bytes 32768 | tf_op jit(solution)/shard_map/all_to_all | solution.py:133
  119.5 38.5 %all-to-all-start.2 = ((bf16[32,16,1024]{2,1,0:T(8,128)(2,1)}), bf16[32,16,1024]{2,1,0:T(8,128)(2,1)S(1)}, u32[]{:S(2)}, u32[]{:S(2)}) async-start(bf16[32,16,1024]{2,1,0:T(8,128)(2,1)} %bitcast.136), calls=%async_computation.2 | async-start | bytes 2097152 | tf_op jit(solution)/shard_map/all_to_all | solution.py:126
  165.9 136.7 %collective-permute-start.6 = (bf16[15,1024]{1,0:T(8,128)(2,1)S(1)}, bf16[15,1024]{1,0:T(8,128)(2,1)S(1)}, u32[]{:S(2)}, u32[]{:S(2)}) collective-permute-start(bf16[15,1024]{1,0:T(8,128)(2,1)S(1)} %get-tuple-element.173), channel_id=1, source_target_pairs={{0,1},{1,2},{2,3},{3,4},{4,5},{5,6},{6,7},{7,8},{8,9},{9,10},{10,1... | collective-permute-start | bytes 92168 | tf_op jit(solution)/shard_map/ppermute | solution.py:14
  167.2 135.4 %collective-permute-start.7 = (bf16[15,1024]{1,0:T(8,128)(2,1)S(1)}, bf16[15,1024]{1,0:T(8,128)(2,1)S(1)}, u32[]{:S(2)}, u32[]{:S(2)}) collective-permute-start(bf16[15,1024]{1,0:T(8,128)(2,1)S(1)} %get-tuple-element.174), channel_id=1, source_target_pairs={{1,0},{2,1},{3,2},{4,3},{5,4},{6,5},{7,6},{8,7},{9,8},{10,9},{11,1... | collective-permute-start | bytes 92168 | tf_op jit(solution)/shard_map/ppermute | solution.py:15
  306.7 12.3 %collective-permute-start = (bf16[128,8,64]{0,2,1:T(8,128)(2,1)S(1)}, bf16[128,8,64]{0,2,1:T(8,128)(2,1)S(1)}, u32[]{:S(2)}, u32[]{:S(2)}) collective-permute-start(bf16[128,8,64]{0,2,1:T(8,128)(2,1)S(1)} %copy.69), channel_id=1, source_target_pairs={{0,1},{1,2},{2,3},{3,4},{4,5},{5,6},{6,7},{7,8},{8,9},{9,10},{10,1... | collective-permute-start | bytes 393224 | tf_op jit(solution)/shard_map/while/body/eval_jaxpr/ppermute | solution.py:23
  307.7 11.3 %collective-permute-start.1 = (bf16[128,8,64]{0,2,1:T(8,128)(2,1)S(1)}, bf16[128,8,64]{0,2,1:T(8,128)(2,1)}, u32[]{:S(2)}, u32[]{:S(2)}) collective-permute-start(bf16[128,8,64]{0,2,1:T(8,128)(2,1)S(1)} %copy.70), channel_id=1, source_target_pairs={{0,1},{1,2},{2,3},{3,4},{4,5},{5,6},{6,7},{7,8},{8,9},{9,10},{10,1... | collective-permute-start | bytes 393224 | tf_op jit(solution)/shard_map/while/body/eval_jaxpr/ppermute | solution.py:23
  319.1 12.3 %collective-permute-start = (bf16[128,8,64]{0,2,1:T(8,128)(2,1)S(1)}, bf16[128,8,64]{0,2,1:T(8,128)(2,1)S(1)}, u32[]{:S(2)}, u32[]{:S(2)}) collective-permute-start(bf16[128,8,64]{0,2,1:T(8,128)(2,1)S(1)} %copy.69), channel_id=1, source_target_pairs={{0,1},{1,2},{2,3},{3,4},{4,5},{5,6},{6,7},{7,8},{8,9},{9,10},{10,1... | collective-permute-start | bytes 393224 | tf_op jit(solution)/shard_map/while/body/eval_jaxpr/ppermute | solution.py:23
  331.5 12.3 %collective-permute-start = (bf16[128,8,64]{0,2,1:T(8,128)(2,1)S(1)}, bf16[128,8,64]{0,2,1:T(8,128)(2,1)S(1)}, u32[]{:S(2)}, u32[]{:S(2)}) collective-permute-start(bf16[128,8,64]{0,2,1:T(8,128)(2,1)S(1)} %copy.69), channel_id=1, source_target_pairs={{0,1},{1,2},{2,3},{3,4},{4,5},{5,6},{6,7},{7,8},{8,9},{9,10},{10,1... | collective-permute-start | bytes 393224 | tf_op jit(solution)/shard_map/while/body/eval_jaxpr/ppermute | solution.py:23
  332.5 11.3 %collective-permute-start.1 = (bf16[128,8,64]{0,2,1:T(8,128)(2,1)S(1)}, bf16[128,8,64]{0,2,1:T(8,128)(2,1)}, u32[]{:S(2)}, u32[]{:S(2)}) collective-permute-start(bf16[128,8,64]{0,2,1:T(8,128)(2,1)S(1)} %copy.70), channel_id=1, source_target_pairs={{0,1},{1,2},{2,3},{3,4},{4,5},{5,6},{6,7},{7,8},{8,9},{9,10},{10,1... | collective-permute-start | bytes 393224 | tf_op jit(solution)/shard_map/while/body/eval_jaxpr/ppermute | solution.py:23
  343.9 12.3 %collective-permute-start = (bf16[128,8,64]{0,2,1:T(8,128)(2,1)S(1)}, bf16[128,8,64]{0,2,1:T(8,128)(2,1)S(1)}, u32[]{:S(2)}, u32[]{:S(2)}) collective-permute-start(bf16[128,8,64]{0,2,1:T(8,128)(2,1)S(1)} %copy.69), channel_id=1, source_target_pairs={{0,1},{1,2},{2,3},{3,4},{4,5},{5,6},{6,7},{7,8},{8,9},{9,10},{10,1... | collective-permute-start | bytes 393224 | tf_op jit(solution)/shard_map/while/body/eval_jaxpr/ppermute | solution.py:23
  344.9 11.3 %collective-permute-start.1 = (bf16[128,8,64]{0,2,1:T(8,128)(2,1)S(1)}, bf16[128,8,64]{0,2,1:T(8,128)(2,1)}, u32[]{:S(2)}, u32[]{:S(2)}) collective-permute-start(bf16[128,8,64]{0,2,1:T(8,128)(2,1)S(1)} %copy.70), channel_id=1, source_target_pairs={{0,1},{1,2},{2,3},{3,4},{4,5},{5,6},{6,7},{7,8},{8,9},{9,10},{10,1... | collective-permute-start | bytes 393224 | tf_op jit(solution)/shard_map/while/body/eval_jaxpr/ppermute | solution.py:23
  356.2 12.3 %collective-permute-start = (bf16[128,8,64]{0,2,1:T(8,128)(2,1)S(1)}, bf16[128,8,64]{0,2,1:T(8,128)(2,1)S(1)}, u32[]{:S(2)}, u32[]{:S(2)}) collective-permute-start(bf16[128,8,64]{0,2,1:T(8,128)(2,1)S(1)} %copy.69), channel_id=1, source_target_pairs={{0,1},{1,2},{2,3},{3,4},{4,5},{5,6},{6,7},{7,8},{8,9},{9,10},{10,1... | collective-permute-start | bytes 393224 | tf_op jit(solution)/shard_map/while/body/eval_jaxpr/ppermute | solution.py:23
  357.2 11.3 %collective-permute-start.1 = (bf16[128,8,64]{0,2,1:T(8,128)(2,1)S(1)}, bf16[128,8,64]{0,2,1:T(8,128)(2,1)}, u32[]{:S(2)}, u32[]{:S(2)}) collective-permute-start(bf16[128,8,64]{0,2,1:T(8,128)(2,1)S(1)} %copy.70), channel_id=1, source_target_pairs={{0,1},{1,2},{2,3},{3,4},{4,5},{5,6},{6,7},{7,8},{8,9},{9,10},{10,1... | collective-permute-start | bytes 393224 | tf_op jit(solution)/shard_map/while/body/eval_jaxpr/ppermute | solution.py:23
  368.6 12.3 %collective-permute-start = (bf16[128,8,64]{0,2,1:T(8,128)(2,1)S(1)}, bf16[128,8,64]{0,2,1:T(8,128)(2,1)S(1)}, u32[]{:S(2)}, u32[]{:S(2)}) collective-permute-start(bf16[128,8,64]{0,2,1:T(8,128)(2,1)S(1)} %copy.69), channel_id=1, source_target_pairs={{0,1},{1,2},{2,3},{3,4},{4,5},{5,6},{6,7},{7,8},{8,9},{9,10},{10,1... | collective-permute-start | bytes 393224 | tf_op jit(solution)/shard_map/while/body/eval_jaxpr/ppermute | solution.py:23
  369.6 11.3 %collective-permute-start.1 = (bf16[128,8,64]{0,2,1:T(8,128)(2,1)S(1)}, bf16[128,8,64]{0,2,1:T(8,128)(2,1)}, u32[]{:S(2)}, u32[]{:S(2)}) collective-permute-start(bf16[128,8,64]{0,2,1:T(8,128)(2,1)S(1)} %copy.70), channel_id=1, source_target_pairs={{0,1},{1,2},{2,3},{3,4},{4,5},{5,6},{6,7},{7,8},{8,9},{9,10},{10,1... | collective-permute-start | bytes 393224 | tf_op jit(solution)/shard_map/while/body/eval_jaxpr/ppermute | solution.py:23
  381.0 15.0 %collective-permute-start = (bf16[128,8,64]{0,2,1:T(8,128)(2,1)S(1)}, bf16[128,8,64]{0,2,1:T(8,128)(2,1)S(1)}, u32[]{:S(2)}, u32[]{:S(2)}) collective-permute-start(bf16[128,8,64]{0,2,1:T(8,128)(2,1)S(1)} %copy.69), channel_id=1, source_target_pairs={{0,1},{1,2},{2,3},{3,4},{4,5},{5,6},{6,7},{7,8},{8,9},{9,10},{10,1... | collective-permute-start | bytes 393224 | tf_op jit(solution)/shard_map/while/body/eval_jaxpr/ppermute | solution.py:23
  382.0 14.0 %collective-permute-start.1 = (bf16[128,8,64]{0,2,1:T(8,128)(2,1)S(1)}, bf16[128,8,64]{0,2,1:T(8,128)(2,1)}, u32[]{:S(2)}, u32[]{:S(2)}) collective-permute-start(bf16[128,8,64]{0,2,1:T(8,128)(2,1)S(1)} %copy.70), channel_id=1, source_target_pairs={{0,1},{1,2},{2,3},{3,4},{4,5},{5,6},{6,7},{7,8},{8,9},{9,10},{10,1... | collective-permute-start | bytes 393224 | tf_op jit(solution)/shard_map/while/body/eval_jaxpr/ppermute | solution.py:23
  396.0 15.4 %collective-permute-start = (bf16[128,8,64]{0,2,1:T(8,128)(2,1)S(1)}, bf16[128,8,64]{0,2,1:T(8,128)(2,1)S(1)}, u32[]{:S(2)}, u32[]{:S(2)}) collective-permute-start(bf16[128,8,64]{0,2,1:T(8,128)(2,1)S(1)} %copy.69), channel_id=1, source_target_pairs={{0,1},{1,2},{2,3},{3,4},{4,5},{5,6},{6,7},{7,8},{8,9},{9,10},{10,1... | collective-permute-start | bytes 393224 | tf_op jit(solution)/shard_map/while/body/eval_jaxpr/ppermute | solution.py:23
  397.0 14.4 %collective-permute-start.1 = (bf16[128,8,64]{0,2,1:T(8,128)(2,1)S(1)}, bf16[128,8,64]{0,2,1:T(8,128)(2,1)}, u32[]{:S(2)}, u32[]{:S(2)}) collective-permute-start(bf16[128,8,64]{0,2,1:T(8,128)(2,1)S(1)} %copy.70), channel_id=1, source_target_pairs={{0,1},{1,2},{2,3},{3,4},{4,5},{5,6},{6,7},{7,8},{8,9},{9,10},{10,1... | collective-permute-start | bytes 393224 | tf_op jit(solution)/shard_map/while/body/eval_jaxpr/ppermute | solution.py:23
  411.4 12.3 %collective-permute-start = (bf16[128,8,64]{0,2,1:T(8,128)(2,1)S(1)}, bf16[128,8,64]{0,2,1:T(8,128)(2,1)S(1)}, u32[]{:S(2)}, u32[]{:S(2)}) collective-permute-start(bf16[128,8,64]{0,2,1:T(8,128)(2,1)S(1)} %copy.69), channel_id=1, source_target_pairs={{0,1},{1,2},{2,3},{3,4},{4,5},{5,6},{6,7},{7,8},{8,9},{9,10},{10,1... | collective-permute-start | bytes 393224 | tf_op jit(solution)/shard_map/while/body/eval_jaxpr/ppermute | solution.py:23
  423.8 12.3 %collective-permute-start = (bf16[128,8,64]{0,2,1:T(8,128)(2,1)S(1)}, bf16[128,8,64]{0,2,1:T(8,128)(2,1)S(1)}, u32[]{:S(2)}, u32[]{:S(2)}) collective-permute-start(bf16[128,8,64]{0,2,1:T(8,128)(2,1)S(1)} %copy.69), channel_id=1, source_target_pairs={{0,1},{1,2},{2,3},{3,4},{4,5},{5,6},{6,7},{7,8},{8,9},{9,10},{10,1... | collective-permute-start | bytes 393224 | tf_op jit(solution)/shard_map/while/body/eval_jaxpr/ppermute | solution.py:23
  436.2 12.3 %collective-permute-start = (bf16[128,8,64]{0,2,1:T(8,128)(2,1)S(1)}, bf16[128,8,64]{0,2,1:T(8,128)(2,1)S(1)}, u32[]{:S(2)}, u32[]{:S(2)}) collective-permute-start(bf16[128,8,64]{0,2,1:T(8,128)(2,1)S(1)} %copy.69), channel_id=1, source_target_pairs={{0,1},{1,2},{2,3},{3,4},{4,5},{5,6},{6,7},{7,8},{8,9},{9,10},{10,1... | collective-permute-start | bytes 393224 | tf_op jit(solution)/shard_map/while/body/eval_jaxpr/ppermute | solution.py:23
  437.2 11.3 %collective-permute-start.1 = (bf16[128,8,64]{0,2,1:T(8,128)(2,1)S(1)}, bf16[128,8,64]{0,2,1:T(8,128)(2,1)}, u32[]{:S(2)}, u32[]{:S(2)}) collective-permute-start(bf16[128,8,64]{0,2,1:T(8,128)(2,1)S(1)} %copy.70), channel_id=1, source_target_pairs={{0,1},{1,2},{2,3},{3,4},{4,5},{5,6},{6,7},{7,8},{8,9},{9,10},{10,1... | collective-permute-start | bytes 393224 | tf_op jit(solution)/shard_map/while/body/eval_jaxpr/ppermute | solution.py:23
  448.6 12.3 %collective-permute-start = (bf16[128,8,64]{0,2,1:T(8,128)(2,1)S(1)}, bf16[128,8,64]{0,2,1:T(8,128)(2,1)S(1)}, u32[]{:S(2)}, u32[]{:S(2)}) collective-permute-start(bf16[128,8,64]{0,2,1:T(8,128)(2,1)S(1)} %copy.69), channel_id=1, source_target_pairs={{0,1},{1,2},{2,3},{3,4},{4,5},{5,6},{6,7},{7,8},{8,9},{9,10},{10,1... | collective-permute-start | bytes 393224 | tf_op jit(solution)/shard_map/while/body/eval_jaxpr/ppermute | solution.py:23
  449.6 11.3 %collective-permute-start.1 = (bf16[128,8,64]{0,2,1:T(8,128)(2,1)S(1)}, bf16[128,8,64]{0,2,1:T(8,128)(2,1)}, u32[]{:S(2)}, u32[]{:S(2)}) collective-permute-start(bf16[128,8,64]{0,2,1:T(8,128)(2,1)S(1)} %copy.70), channel_id=1, source_target_pairs={{0,1},{1,2},{2,3},{3,4},{4,5},{5,6},{6,7},{7,8},{8,9},{9,10},{10,1... | collective-permute-start | bytes 393224 | tf_op jit(solution)/shard_map/while/body/eval_jaxpr/ppermute | solution.py:23
  460.9 12.3 %collective-permute-start = (bf16[128,8,64]{0,2,1:T(8,128)(2,1)S(1)}, bf16[128,8,64]{0,2,1:T(8,128)(2,1)S(1)}, u32[]{:S(2)}, u32[]{:S(2)}) collective-permute-start(bf16[128,8,64]{0,2,1:T(8,128)(2,1)S(1)} %copy.69), channel_id=1, source_target_pairs={{0,1},{1,2},{2,3},{3,4},{4,5},{5,6},{6,7},{7,8},{8,9},{9,10},{10,1... | collective-permute-start | bytes 393224 | tf_op jit(solution)/shard_map/while/body/eval_jaxpr/ppermute | solution.py:23
  461.9 11.3 %collective-permute-start.1 = (bf16[128,8,64]{0,2,1:T(8,128)(2,1)S(1)}, bf16[128,8,64]{0,2,1:T(8,128)(2,1)}, u32[]{:S(2)}, u32[]{:S(2)}) collective-permute-start(bf16[128,8,64]{0,2,1:T(8,128)(2,1)S(1)} %copy.70), channel_id=1, source_target_pairs={{0,1},{1,2},{2,3},{3,4},{4,5},{5,6},{6,7},{7,8},{8,9},{9,10},{10,1... | collective-permute-start | bytes 393224 | tf_op jit(solution)/shard_map/while/body/eval_jaxpr/ppermute | solution.py:23
  473.3 12.3 %collective-permute-start = (bf16[128,8,64]{0,2,1:T(8,128)(2,1)S(1)}, bf16[128,8,64]{0,2,1:T(8,128)(2,1)S(1)}, u32[]{:S(2)}, u32[]{:S(2)}) collective-permute-start(bf16[128,8,64]{0,2,1:T(8,128)(2,1)S(1)} %copy.69), channel_id=1, source_target_pairs={{0,1},{1,2},{2,3},{3,4},{4,5},{5,6},{6,7},{7,8},{8,9},{9,10},{10,1... | collective-permute-start | bytes 393224 | tf_op jit(solution)/shard_map/while/body/eval_jaxpr/ppermute | solution.py:23
  474.3 11.3 %collective-permute-start.1 = (bf16[128,8,64]{0,2,1:T(8,128)(2,1)S(1)}, bf16[128,8,64]{0,2,1:T(8,128)(2,1)}, u32[]{:S(2)}, u32[]{:S(2)}) collective-permute-start(bf16[128,8,64]{0,2,1:T(8,128)(2,1)S(1)} %copy.70), channel_id=1, source_target_pairs={{0,1},{1,2},{2,3},{3,4},{4,5},{5,6},{6,7},{7,8},{8,9},{9,10},{10,1... | collective-permute-start | bytes 393224 | tf_op jit(solution)/shard_map/while/body/eval_jaxpr/ppermute | solution.py:23
  485.7 12.3 %collective-permute-start = (bf16[128,8,64]{0,2,1:T(8,128)(2,1)S(1)}, bf16[128,8,64]{0,2,1:T(8,128)(2,1)S(1)}, u32[]{:S(2)}, u32[]{:S(2)}) collective-permute-start(bf16[128,8,64]{0,2,1:T(8,128)(2,1)S(1)} %copy.69), channel_id=1, source_target_pairs={{0,1},{1,2},{2,3},{3,4},{4,5},{5,6},{6,7},{7,8},{8,9},{9,10},{10,1... | collective-permute-start | bytes 393224 | tf_op jit(solution)/shard_map/while/body/eval_jaxpr/ppermute | solution.py:23
  486.7 11.3 %collective-permute-start.1 = (bf16[128,8,64]{0,2,1:T(8,128)(2,1)S(1)}, bf16[128,8,64]{0,2,1:T(8,128)(2,1)}, u32[]{:S(2)}, u32[]{:S(2)}) collective-permute-start(bf16[128,8,64]{0,2,1:T(8,128)(2,1)S(1)} %copy.70), channel_id=1, source_target_pairs={{0,1},{1,2},{2,3},{3,4},{4,5},{5,6},{6,7},{7,8},{8,9},{9,10},{10,1... | collective-permute-start | bytes 393224 | tf_op jit(solution)/shard_map/while/body/eval_jaxpr/ppermute | solution.py:23
  498.1 15.0 %collective-permute-start = (bf16[128,8,64]{0,2,1:T(8,128)(2,1)S(1)}, bf16[128,8,64]{0,2,1:T(8,128)(2,1)S(1)}, u32[]{:S(2)}, u32[]{:S(2)}) collective-permute-start(bf16[128,8,64]{0,2,1:T(8,128)(2,1)S(1)} %copy.69), channel_id=1, source_target_pairs={{0,1},{1,2},{2,3},{3,4},{4,5},{5,6},{6,7},{7,8},{8,9},{9,10},{10,1... | collective-permute-start | bytes 393224 | tf_op jit(solution)/shard_map/while/body/eval_jaxpr/ppermute | solution.py:23
  499.1 14.0 %collective-permute-start.1 = (bf16[128,8,64]{0,2,1:T(8,128)(2,1)S(1)}, bf16[128,8,64]{0,2,1:T(8,128)(2,1)}, u32[]{:S(2)}, u32[]{:S(2)}) collective-permute-start(bf16[128,8,64]{0,2,1:T(8,128)(2,1)S(1)} %copy.70), channel_id=1, source_target_pairs={{0,1},{1,2},{2,3},{3,4},{4,5},{5,6},{6,7},{7,8},{8,9},{9,10},{10,1... | collective-permute-start | bytes 393224 | tf_op jit(solution)/shard_map/while/body/eval_jaxpr/ppermute | solution.py:23
  513.1 12.3 %collective-permute-start = (bf16[128,8,64]{0,2,1:T(8,128)(2,1)S(1)}, bf16[128,8,64]{0,2,1:T(8,128)(2,1)S(1)}, u32[]{:S(2)}, u32[]{:S(2)}) collective-permute-start(bf16[128,8,64]{0,2,1:T(8,128)(2,1)S(1)} %copy.69), channel_id=1, source_target_pairs={{0,1},{1,2},{2,3},{3,4},{4,5},{5,6},{6,7},{7,8},{8,9},{9,10},{10,1... | collective-permute-start | bytes 393224 | tf_op jit(solution)/shard_map/while/body/eval_jaxpr/ppermute | solution.py:23
  514.1 11.3 %collective-permute-start.1 = (bf16[128,8,64]{0,2,1:T(8,128)(2,1)S(1)}, bf16[128,8,64]{0,2,1:T(8,128)(2,1)}, u32[]{:S(2)}, u32[]{:S(2)}) collective-permute-start(bf16[128,8,64]{0,2,1:T(8,128)(2,1)S(1)} %copy.70), channel_id=1, source_target_pairs={{0,1},{1,2},{2,3},{3,4},{4,5},{5,6},{6,7},{7,8},{8,9},{9,10},{10,1... | collective-permute-start | bytes 393224 | tf_op jit(solution)/shard_map/while/body/eval_jaxpr/ppermute | solution.py:23
  525.5 12.3 %collective-permute-start = (bf16[128,8,64]{0,2,1:T(8,128)(2,1)S(1)}, bf16[128,8,64]{0,2,1:T(8,128)(2,1)S(1)}, u32[]{:S(2)}, u32[]{:S(2)}) collective-permute-start(bf16[128,8,64]{0,2,1:T(8,128)(2,1)S(1)} %copy.69), channel_id=1, source_target_pairs={{0,1},{1,2},{2,3},{3,4},{4,5},{5,6},{6,7},{7,8},{8,9},{9,10},{10,1... | collective-permute-start | bytes 393224 | tf_op jit(solution)/shard_map/while/body/eval_jaxpr/ppermute | solution.py:23
  526.5 11.3 %collective-permute-start.1 = (bf16[128,8,64]{0,2,1:T(8,128)(2,1)S(1)}, bf16[128,8,64]{0,2,1:T(8,128)(2,1)}, u32[]{:S(2)}, u32[]{:S(2)}) collective-permute-start(bf16[128,8,64]{0,2,1:T(8,128)(2,1)S(1)} %copy.70), channel_id=1, source_target_pairs={{0,1},{1,2},{2,3},{3,4},{4,5},{5,6},{6,7},{7,8},{8,9},{9,10},{10,1... | collective-permute-start | bytes 393224 | tf_op jit(solution)/shard_map/while/body/eval_jaxpr/ppermute | solution.py:23
  537.8 12.3 %collective-permute-start = (bf16[128,8,64]{0,2,1:T(8,128)(2,1)S(1)}, bf16[128,8,64]{0,2,1:T(8,128)(2,1)S(1)}, u32[]{:S(2)}, u32[]{:S(2)}) collective-permute-start(bf16[128,8,64]{0,2,1:T(8,128)(2,1)S(1)} %copy.69), channel_id=1, source_target_pairs={{0,1},{1,2},{2,3},{3,4},{4,5},{5,6},{6,7},{7,8},{8,9},{9,10},{10,1... | collective-permute-start | bytes 393224 | tf_op jit(solution)/shard_map/while/body/eval_jaxpr/ppermute | solution.py:23
  538.8 11.3 %collective-permute-start.1 = (bf16[128,8,64]{0,2,1:T(8,128)(2,1)S(1)}, bf16[128,8,64]{0,2,1:T(8,128)(2,1)}, u32[]{:S(2)}, u32[]{:S(2)}) collective-permute-start(bf16[128,8,64]{0,2,1:T(8,128)(2,1)S(1)} %copy.70), channel_id=1, source_target_pairs={{0,1},{1,2},{2,3},{3,4},{4,5},{5,6},{6,7},{7,8},{8,9},{9,10},{10,1... | collective-permute-start | bytes 393224 | tf_op jit(solution)/shard_map/while/body/eval_jaxpr/ppermute | solution.py:23
  550.2 12.3 %collective-permute-start = (bf16[128,8,64]{0,2,1:T(8,128)(2,1)S(1)}, bf16[128,8,64]{0,2,1:T(8,128)(2,1)S(1)}, u32[]{:S(2)}, u32[]{:S(2)}) collective-permute-start(bf16[128,8,64]{0,2,1:T(8,128)(2,1)S(1)} %copy.69), channel_id=1, source_target_pairs={{0,1},{1,2},{2,3},{3,4},{4,5},{5,6},{6,7},{7,8},{8,9},{9,10},{10,1... | collective-permute-start | bytes 393224 | tf_op jit(solution)/shard_map/while/body/eval_jaxpr/ppermute | solution.py:23
  551.2 11.3 %collective-permute-start.1 = (bf16[128,8,64]{0,2,1:T(8,128)(2,1)S(1)}, bf16[128,8,64]{0,2,1:T(8,128)(2,1)}, u32[]{:S(2)}, u32[]{:S(2)}) collective-permute-start(bf16[128,8,64]{0,2,1:T(8,128)(2,1)S(1)} %copy.70), channel_id=1, source_target_pairs={{0,1},{1,2},{2,3},{3,4},{4,5},{5,6},{6,7},{7,8},{8,9},{9,10},{10,1... | collective-permute-start | bytes 393224 | tf_op jit(solution)/shard_map/while/body/eval_jaxpr/ppermute | solution.py:23
  562.6 12.3 %collective-permute-start = (bf16[128,8,64]{0,2,1:T(8,128)(2,1)S(1)}, bf16[128,8,64]{0,2,1:T(8,128)(2,1)S(1)}, u32[]{:S(2)}, u32[]{:S(2)}) collective-permute-start(bf16[128,8,64]{0,2,1:T(8,128)(2,1)S(1)} %copy.69), channel_id=1, source_target_pairs={{0,1},{1,2},{2,3},{3,4},{4,5},{5,6},{6,7},{7,8},{8,9},{9,10},{10,1... | collective-permute-start | bytes 393224 | tf_op jit(solution)/shard_map/while/body/eval_jaxpr/ppermute | solution.py:23
  563.6 11.3 %collective-permute-start.1 = (bf16[128,8,64]{0,2,1:T(8,128)(2,1)S(1)}, bf16[128,8,64]{0,2,1:T(8,128)(2,1)}, u32[]{:S(2)}, u32[]{:S(2)}) collective-permute-start(bf16[128,8,64]{0,2,1:T(8,128)(2,1)S(1)} %copy.70), channel_id=1, source_target_pairs={{0,1},{1,2},{2,3},{3,4},{4,5},{5,6},{6,7},{7,8},{8,9},{9,10},{10,1... | collective-permute-start | bytes 393224 | tf_op jit(solution)/shard_map/while/body/eval_jaxpr/ppermute | solution.py:23
  575.0 12.3 %collective-permute-start = (bf16[128,8,64]{0,2,1:T(8,128)(2,1)S(1)}, bf16[128,8,64]{0,2,1:T(8,128)(2,1)S(1)}, u32[]{:S(2)}, u32[]{:S(2)}) collective-permute-start(bf16[128,8,64]{0,2,1:T(8,128)(2,1)S(1)} %copy.69), channel_id=1, source_target_pairs={{0,1},{1,2},{2,3},{3,4},{4,5},{5,6},{6,7},{7,8},{8,9},{9,10},{10,1... | collective-permute-start | bytes 393224 | tf_op jit(solution)/shard_map/while/body/eval_jaxpr/ppermute | solution.py:23
  575.9 11.3 %collective-permute-start.1 = (bf16[128,8,64]{0,2,1:T(8,128)(2,1)S(1)}, bf16[128,8,64]{0,2,1:T(8,128)(2,1)}, u32[]{:S(2)}, u32[]{:S(2)}) collective-permute-start(bf16[128,8,64]{0,2,1:T(8,128)(2,1)S(1)} %copy.70), channel_id=1, source_target_pairs={{0,1},{1,2},{2,3},{3,4},{4,5},{5,6},{6,7},{7,8},{8,9},{9,10},{10,1... | collective-permute-start | bytes 393224 | tf_op jit(solution)/shard_map/while/body/eval_jaxpr/ppermute | solution.py:23
  587.3 15.0 %collective-permute-start = (bf16[128,8,64]{0,2,1:T(8,128)(2,1)S(1)}, bf16[128,8,64]{0,2,1:T(8,128)(2,1)S(1)}, u32[]{:S(2)}, u32[]{:S(2)}) collective-permute-start(bf16[128,8,64]{0,2,1:T(8,128)(2,1)S(1)} %copy.69), channel_id=1, source_target_pairs={{0,1},{1,2},{2,3},{3,4},{4,5},{5,6},{6,7},{7,8},{8,9},{9,10},{10,1... | collective-permute-start | bytes 393224 | tf_op jit(solution)/shard_map/while/body/eval_jaxpr/ppermute | solution.py:23
  588.3 14.0 %collective-permute-start.1 = (bf16[128,8,64]{0,2,1:T(8,128)(2,1)S(1)}, bf16[128,8,64]{0,2,1:T(8,128)(2,1)}, u32[]{:S(2)}, u32[]{:S(2)}) collective-permute-start(bf16[128,8,64]{0,2,1:T(8,128)(2,1)S(1)} %copy.70), channel_id=1, source_target_pairs={{0,1},{1,2},{2,3},{3,4},{4,5},{5,6},{6,7},{7,8},{8,9},{9,10},{10,1... | collective-permute-start | bytes 393224 | tf_op jit(solution)/shard_map/while/body/eval_jaxpr/ppermute | solution.py:23
  602.4 15.4 %collective-permute-start = (bf16[128,8,64]{0,2,1:T(8,128)(2,1)S(1)}, bf16[128,8,64]{0,2,1:T(8,128)(2,1)S(1)}, u32[]{:S(2)}, u32[]{:S(2)}) collective-permute-start(bf16[128,8,64]{0,2,1:T(8,128)(2,1)S(1)} %copy.69), channel_id=1, source_target_pairs={{0,1},{1,2},{2,3},{3,4},{4,5},{5,6},{6,7},{7,8},{8,9},{9,10},{10,1... | collective-permute-start | bytes 393224 | tf_op jit(solution)/shard_map/while/body/eval_jaxpr/ppermute | solution.py:23
  603.4 14.4 %collective-permute-start.1 = (bf16[128,8,64]{0,2,1:T(8,128)(2,1)S(1)}, bf16[128,8,64]{0,2,1:T(8,128)(2,1)}, u32[]{:S(2)}, u32[]{:S(2)}) collective-permute-start(bf16[128,8,64]{0,2,1:T(8,128)(2,1)S(1)} %copy.70), channel_id=1, source_target_pairs={{0,1},{1,2},{2,3},{3,4},{4,5},{5,6},{6,7},{7,8},{8,9},{9,10},{10,1... | collective-permute-start | bytes 393224 | tf_op jit(solution)/shard_map/while/body/eval_jaxpr/ppermute | solution.py:23
  617.8 12.3 %collective-permute-start = (bf16[128,8,64]{0,2,1:T(8,128)(2,1)S(1)}, bf16[128,8,64]{0,2,1:T(8,128)(2,1)S(1)}, u32[]{:S(2)}, u32[]{:S(2)}) collective-permute-start(bf16[128,8,64]{0,2,1:T(8,128)(2,1)S(1)} %copy.69), channel_id=1, source_target_pairs={{0,1},{1,2},{2,3},{3,4},{4,5},{5,6},{6,7},{7,8},{8,9},{9,10},{10,1... | collective-permute-start | bytes 393224 | tf_op jit(solution)/shard_map/while/body/eval_jaxpr/ppermute | solution.py:23
  618.8 11.3 %collective-permute-start.1 = (bf16[128,8,64]{0,2,1:T(8,128)(2,1)S(1)}, bf16[128,8,64]{0,2,1:T(8,128)(2,1)}, u32[]{:S(2)}, u32[]{:S(2)}) collective-permute-start(bf16[128,8,64]{0,2,1:T(8,128)(2,1)S(1)} %copy.70), channel_id=1, source_target_pairs={{0,1},{1,2},{2,3},{3,4},{4,5},{5,6},{6,7},{7,8},{8,9},{9,10},{10,1... | collective-permute-start | bytes 393224 | tf_op jit(solution)/shard_map/while/body/eval_jaxpr/ppermute | solution.py:23
  630.2 12.3 %collective-permute-start = (bf16[128,8,64]{0,2,1:T(8,128)(2,1)S(1)}, bf16[128,8,64]{0,2,1:T(8,128)(2,1)S(1)}, u32[]{:S(2)}, u32[]{:S(2)}) collective-permute-start(bf16[128,8,64]{0,2,1:T(8,128)(2,1)S(1)} %copy.69), channel_id=1, source_target_pairs={{0,1},{1,2},{2,3},{3,4},{4,5},{5,6},{6,7},{7,8},{8,9},{9,10},{10,1... | collective-permute-start | bytes 393224 | tf_op jit(solution)/shard_map/while/body/eval_jaxpr/ppermute | solution.py:23
  631.1 11.3 %collective-permute-start.1 = (bf16[128,8,64]{0,2,1:T(8,128)(2,1)S(1)}, bf16[128,8,64]{0,2,1:T(8,128)(2,1)}, u32[]{:S(2)}, u32[]{:S(2)}) collective-permute-start(bf16[128,8,64]{0,2,1:T(8,128)(2,1)S(1)} %copy.70), channel_id=1, source_target_pairs={{0,1},{1,2},{2,3},{3,4},{4,5},{5,6},{6,7},{7,8},{8,9},{9,10},{10,1... | collective-permute-start | bytes 393224 | tf_op jit(solution)/shard_map/while/body/eval_jaxpr/ppermute | solution.py:23
  642.5 12.3 %collective-permute-start = (bf16[128,8,64]{0,2,1:T(8,128)(2,1)S(1)}, bf16[128,8,64]{0,2,1:T(8,128)(2,1)S(1)}, u32[]{:S(2)}, u32[]{:S(2)}) collective-permute-start(bf16[128,8,64]{0,2,1:T(8,128)(2,1)S(1)} %copy.69), channel_id=1, source_target_pairs={{0,1},{1,2},{2,3},{3,4},{4,5},{5,6},{6,7},{7,8},{8,9},{9,10},{10,1... | collective-permute-start | bytes 393224 | tf_op jit(solution)/shard_map/while/body/eval_jaxpr/ppermute | solution.py:23
  643.5 11.3 %collective-permute-start.1 = (bf16[128,8,64]{0,2,1:T(8,128)(2,1)S(1)}, bf16[128,8,64]{0,2,1:T(8,128)(2,1)}, u32[]{:S(2)}, u32[]{:S(2)}) collective-permute-start(bf16[128,8,64]{0,2,1:T(8,128)(2,1)S(1)} %copy.70), channel_id=1, source_target_pairs={{0,1},{1,2},{2,3},{3,4},{4,5},{5,6},{6,7},{7,8},{8,9},{9,10},{10,1... | collective-permute-start | bytes 393224 | tf_op jit(solution)/shard_map/while/body/eval_jaxpr/ppermute | solution.py:23
  654.9 12.3 %collective-permute-start = (bf16[128,8,64]{0,2,1:T(8,128)(2,1)S(1)}, bf16[128,8,64]{0,2,1:T(8,128)(2,1)S(1)}, u32[]{:S(2)}, u32[]{:S(2)}) collective-permute-start(bf16[128,8,64]{0,2,1:T(8,128)(2,1)S(1)} %copy.69), channel_id=1, source_target_pairs={{0,1},{1,2},{2,3},{3,4},{4,5},{5,6},{6,7},{7,8},{8,9},{9,10},{10,1... | collective-permute-start | bytes 393224 | tf_op jit(solution)/shard_map/while/body/eval_jaxpr/ppermute | solution.py:23
  667.3 12.3 %collective-permute-start = (bf16[128,8,64]{0,2,1:T(8,128)(2,1)S(1)}, bf16[128,8,64]{0,2,1:T(8,128)(2,1)S(1)}, u32[]{:S(2)}, u32[]{:S(2)}) collective-permute-start(bf16[128,8,64]{0,2,1:T(8,128)(2,1)S(1)} %copy.69), channel_id=1, source_target_pairs={{0,1},{1,2},{2,3},{3,4},{4,5},{5,6},{6,7},{7,8},{8,9},{9,10},{10,1... | collective-permute-start | bytes 393224 | tf_op jit(solution)/shard_map/while/body/eval_jaxpr/ppermute | solution.py:23
  679.7 12.3 %collective-permute-start = (bf16[128,8,64]{0,2,1:T(8,128)(2,1)S(1)}, bf16[128,8,64]{0,2,1:T(8,128)(2,1)S(1)}, u32[]{:S(2)}, u32[]{:S(2)}) collective-permute-start(bf16[128,8,64]{0,2,1:T(8,128)(2,1)S(1)} %copy.69), channel_id=1, source_target_pairs={{0,1},{1,2},{2,3},{3,4},{4,5},{5,6},{6,7},{7,8},{8,9},{9,10},{10,1... | collective-permute-start | bytes 393224 | tf_op jit(solution)/shard_map/while/body/eval_jaxpr/ppermute | solution.py:23
  692.0 12.3 %collective-permute-start = (bf16[128,8,64]{0,2,1:T(8,128)(2,1)S(1)}, bf16[128,8,64]{0,2,1:T(8,128)(2,1)S(1)}, u32[]{:S(2)}, u32[]{:S(2)}) collective-permute-start(bf16[128,8,64]{0,2,1:T(8,128)(2,1)S(1)} %copy.69), channel_id=1, source_target_pairs={{0,1},{1,2},{2,3},{3,4},{4,5},{5,6},{6,7},{7,8},{8,9},{9,10},{10,1... | collective-permute-start | bytes 393224 | tf_op jit(solution)/shard_map/while/body/eval_jaxpr/ppermute | solution.py:23
  693.0 11.3 %collective-permute-start.1 = (bf16[128,8,64]{0,2,1:T(8,128)(2,1)S(1)}, bf16[128,8,64]{0,2,1:T(8,128)(2,1)}, u32[]{:S(2)}, u32[]{:S(2)}) collective-permute-start(bf16[128,8,64]{0,2,1:T(8,128)(2,1)S(1)} %copy.70), channel_id=1, source_target_pairs={{0,1},{1,2},{2,3},{3,4},{4,5},{5,6},{6,7},{7,8},{8,9},{9,10},{10,1... | collective-permute-start | bytes 393224 | tf_op jit(solution)/shard_map/while/body/eval_jaxpr/ppermute | solution.py:23
  704.4 14.9 %collective-permute-start = (bf16[128,8,64]{0,2,1:T(8,128)(2,1)S(1)}, bf16[128,8,64]{0,2,1:T(8,128)(2,1)S(1)}, u32[]{:S(2)}, u32[]{:S(2)}) collective-permute-start(bf16[128,8,64]{0,2,1:T(8,128)(2,1)S(1)} %copy.69), channel_id=1, source_target_pairs={{0,1},{1,2},{2,3},{3,4},{4,5},{5,6},{6,7},{7,8},{8,9},{9,10},{10,1... | collective-permute-start | bytes 393224 | tf_op jit(solution)/shard_map/while/body/eval_jaxpr/ppermute | solution.py:23
  705.4 14.0 %collective-permute-start.1 = (bf16[128,8,64]{0,2,1:T(8,128)(2,1)S(1)}, bf16[128,8,64]{0,2,1:T(8,128)(2,1)}, u32[]{:S(2)}, u32[]{:S(2)}) collective-permute-start(bf16[128,8,64]{0,2,1:T(8,128)(2,1)S(1)} %copy.70), channel_id=1, source_target_pairs={{0,1},{1,2},{2,3},{3,4},{4,5},{5,6},{6,7},{7,8},{8,9},{9,10},{10,1... | collective-permute-start | bytes 393224 | tf_op jit(solution)/shard_map/while/body/eval_jaxpr/ppermute | solution.py:23
  (144 other events, 5475.8 us)
where the time goes:
time: 723 us; the launch traced here: 722 us
  waiting for transfers between devices  259 us (36%)
  starting transfers between devices  143 us (20%)
  blocking collectives  133 us (18%)
  matrix products  110 us (15%)
  local copies, waits for them, and re-layouts  56.9 us (8%)
  other arithmetic  14 us (2%)
    ppermute x128, waiting for transfers between devices, from_behind(): return lax.ppermute(value, axis, pairs)  191 us
    psum x1, blocking collectives, on_device(): lax.psum(local_terms.astype(jnp.bfloat16), 'ctx').astype(jnp.float32)  133 us
    ppermute x128, starting transfers between devices, from_behind(): return lax.ppermute(value, axis, pairs)  103 us
    while x64, local copies, waits for them, and re-layouts  29.3 us
    dot_general x32, matrix products, key_terms(): jnp.einsum('hqk,qhd->khd', softmax_low, dout_rows, preferred_element_type...  28 us
    dot_general x32, matrix products, key_terms(): jnp.einsum('hqk,qhd->khd', dscores, query_rows, preferred_element_type=jn...  27.9 us
    all_to_all x1, waiting for transfers between devices, on_device(): lax.all_to_all(send_rows, 'ctx', split_axis=0, concat_axis=0, tiled=True)  26.3 us
    all_to_all x1, waiting for transfers between devices, on_device(): lax.all_to_all(send_grads, 'ctx', split_axis=0, concat_axis=0, tiled=True)  22.6 us
  transfers between devices with their start and end apart: 136, of which 68 were waited for; matrix products, arithmetic and copies ran while one was open for 21% of the time, Pallas kernels for 0%

commit v1 on v0

v1 whole, which is shorter than its diff:
```python
import jax
import jax.numpy as jnp
from jax import lax
from jax.experimental import pallas as pl
from jax.experimental.pallas import tpu as pltpu
from jax.sharding import PartitionSpec as P

MESH = pl.DeviceIdType.MESH
F32 = jnp.float32
BF16 = jnp.bfloat16

FR = 128
D = 1024
HEADS = 8
HID = 2048
TAPS = 31
CAP = 16
EXPERTS = 32
ROWS = EXPERTS * CAP
KEYS = 4096

S_G, S_X, S_R, S_T = 0, 32, 64, 96
S_HM, S_HG = 128, 130
S_Q, S_KV, S_KVP = 132, 140, 148
S_DO, S_DKVP, S_DKVZ, S_DQ = 152, 160, 164, 172
S_DC1, S_DC2, S_DC3 = 180, 188, 192
SEMS = 200

NT = (((1,), (1,)), ((), ()))


def dot(a, b):
    return jnp.dot(a, b, preferred_element_type=F32)


def dot_nt(a, b):
    return lax.dot_general(a, b, NT, preferred_element_type=F32)


def rem(a, b):
    return lax.rem(a, jnp.int32(b))


def div(a, b):
    return lax.div(a, jnp.int32(b))


def three_rows(rows, h):
    high = rows[h : h + 1, :].astype(BF16).astype(F32)
    rest = rows[h : h + 1, :] - high
    middle = rest.astype(BF16).astype(F32)
    low = rest - middle
    at = lax.broadcasted_iota(jnp.int32, (16, rows.shape[1]), 0)
    zero = jnp.zeros((16, rows.shape[1]), F32)
    block = jnp.where(at == 0, high, jnp.where(at == 1, middle, jnp.where(at == 2, low, zero)))
    return block.astype(BF16)


def lanes_below(shape, n):
    return lax.broadcasted_iota(jnp.int32, shape, 1) < n


def kernel(
    mid_ref, up_ref, q_ref, k_ref, v_ref, attn_ref, norm_ref, oproj_hbm, cw_ref, gates_ref, ids_ref,
    slots_ref, win_hbm, wout_hbm,
    dmid_ref, dq_ref, dk_ref, dv_ref, dconv_ref, dgates_ref,
    win, wout, oproj, wide, gwide, cwf, halo_m, halo_g, gm, pick, sg, sx, rg, rx, upw, hg, rs, rr,
    gs, gr, g2, qs, qr, ks, kva, qz, qn, nrow, kt, pt, dos, dor, doz, don, drow, attn_t, dkv_s, dkv_r,
    dkv0, dkv_z, dkv_o, dqa, dq_s, dq_o, dc_s, dc_r, dc1, dc2, dc3, dcf, tmp,
    ssem, rsem, wsem,
):
    grp, ctx = lax.axis_index("grp"), lax.axis_index("ctx")
    ylo, xx = div(grp, 4), rem(grp, 4)
    z, yhi, core = div(ctx, 4), rem(div(ctx, 2), 2), rem(ctx, 2)
    j = rem(ctx, 4)

    def near(dz, dj, in_group=False):
        dz, dj = jnp.int32(dz), jnp.int32(dj)
        dy, dc = div(dj, 2), rem(dj, 2)
        y_other = ylo if in_group else rem(ylo + dy, 2)
        return (
            y_other * 4 + xx,
            rem(z + dz, 8) * 4 + rem(yhi + dy, 2) * 2 + rem(core + dc, 2),
        )

    def along(step):
        return (grp, rem(ctx + step + 32, 32))

    def remote(src, dst, send_at, recv_at, device):
        return pltpu.make_async_remote_copy(
            src_ref=src, dst_ref=dst, send_sem=ssem.at[send_at], recv_sem=rsem.at[recv_at],
            device_id=device, device_id_type=MESH,
        )

    def arrived(ref, recv_at):
        remote(ref, ref, 0, recv_at, along(1)).wait_recv()

    def sent(ref, send_at):
        remote(ref, ref, send_at, 0, along(1)).wait_send()

    def place(k):
        n = div(k, 4)
        odd = rem(n, 2)
        return rem(odd * div(n + 1, 2) + (1 - odd) * (8 - div(n, 2)), 8), rem(k, 4)

    def slot_rows(k):
        return pl.ds(pl.multiple_of(k * CAP, CAP), CAP)

    w_copies = [
        pltpu.make_async_copy(wout_hbm.at[0], wout, wsem.at[0]),
        pltpu.make_async_copy(win_hbm.at[0], win, wsem.at[1]),
        pltpu.make_async_copy(oproj_hbm, oproj, wsem.at[2]),
    ]
    barrier = pltpu.get_barrier_semaphore()

    def greet(k, _):
        dz, dj = place(k)
        pl.semaphore_signal(barrier, inc=1, device_id=near(dz, dj), device_id_type=MESH)
        return 0

    lax.fori_loop(1, 32, greet, 0)
    for dj in (2, 3):
        pl.semaphore_signal(barrier, inc=1, device_id=near(0, dj, True), device_id_type=MESH)
    for step in (1, -1):
        pl.semaphore_signal(barrier, inc=1, device_id=along(step), device_id_type=MESH)
    for copy in w_copies:
        copy.start()

    ids, slot = ids_ref[...], slots_ref[...]
    planes_on = (jnp.right_shift(ids, 2) - z + 8) & 7
    in_plane = ((jnp.right_shift(ids, 1) + yhi) & 1) * 2 + ((ids + core) & 1)
    spot = planes_on * 4 + in_plane
    sid = spot * CAP + slot
    lane = lax.broadcasted_iota(jnp.int32, (FR, ROWS), 1)
    both = jnp.zeros((FR, ROWS), F32)
    for r in range(2):
        hit = jnp.where(lane == sid[:, r : r + 1], 1.0, 0.0).astype(F32)
        pick[r] = hit.astype(BF16)
        both = both + hit
    spread = jnp.transpose(both).astype(BF16)

    for n in range(4):
        rows = slice(n * 128, n * 128 + 128)
        sg[rows, :] = dot(spread[rows, :], up_ref[...]).astype(BF16)
    rg[0:CAP, :] = sg[0:CAP, :]

    pl.semaphore_wait(barrier, 35)

    halo_m_out = [
        remote(mid_ref.at[pl.ds(FR - 16, 16)], halo_m.at[0], S_HM, S_HM, along(1)),
        remote(mid_ref.at[pl.ds(0, 16)], halo_m.at[1], S_HM + 1, S_HM + 1, along(-1)),
    ]
    for copy in halo_m_out:
        copy.start()

    def spread_out(src, dst, first):
        def body(k, _):
            dz, dj = place(k)
            here = dz * 4 + dj
            there = rem(8 - dz, 8) * 4 + dj
            remote(
                src.at[slot_rows(here)], dst.at[slot_rows(there)], first + here, first + there, near(dz, dj)
            ).start()
            return 0

        lax.fori_loop(1, 32, body, 0)

    spread_out(sg, rg, S_G)

    cwf[0:TAPS, :] = cw_ref[...].astype(F32)
    tmp[...] = jnp.zeros((FR, 128), F32)
    tmp[:, 0:HEADS] = norm_ref[...]
    norm_t = jnp.transpose(tmp[...])
    for n in range(4):
        cols = slice(n * 128, n * 128 + 128)
        q_t = jnp.transpose(q_ref[:, cols].astype(F32) * 0.125).astype(BF16)
        attn_t[cols, :] = jnp.transpose(attn_ref[:, cols].astype(F32))
        kk, vv = k_ref[:, cols].astype(F32), v_ref[:, cols].astype(F32)
        first = lanes_below((FR, 128), 64)
        ks[2 * n] = jnp.where(first, kk, pltpu.roll(vv, 64, 1)).astype(BF16)
        ks[2 * n + 1] = jnp.where(first, pltpu.roll(kk, 64, 1), vv).astype(BF16)
        for half in range(2):
            h = 2 * n + half
            qs[h * 80 : h * 80 + 64, :] = q_t[half * 64 : half * 64 + 64, :]
            qs[h * 80 + 64 : h * 80 + 80, :] = three_rows(norm_t, h)

    def head_rows(h):
        return pl.ds(pl.multiple_of(h * 80, 16), 80)

    wide[16 : 16 + FR, :] = mid_ref[...].astype(F32)
    for side, copy in enumerate(halo_m_out):
        arrived(halo_m.at[side], S_HM + side)
    not_first = jnp.where(ctx > 0, 1.0, 0.0).astype(F32)
    not_last = jnp.where(ctx < 31, 1.0, 0.0).astype(F32)
    wide[0:16, :] = halo_m[0].astype(F32) * not_first
    wide[16 + FR : 32 + FR, :] = halo_m[1].astype(F32) * not_last

    def lane_tile(i):
        return pl.ds(pl.multiple_of(i * 128, 128), 128)

    def convolve(src, dst, backward):
        def body(i, _):
            cols = lane_tile(i)
            total = src[pl.ds(16, FR), cols]
            for o in range(1, TAPS + 1):
                tap = TAPS - o if backward else o - 1
                total = total + cwf[pl.ds(tap, 1), cols] * src[pl.ds(o, FR), cols]
            dst[:, cols] = total.astype(BF16)
            return 0

        lax.fori_loop(0, 8, body, 0)

    convolve(wide, gm, False)
    for n in range(4):
        rows = slice(n * 128, n * 128 + 128)
        sx[rows, :] = dot(spread[rows, :], gm[...]).astype(BF16)
    rx[0:CAP, :] = sx[0:CAP, :]
    spread_out(sx, rx, S_X)

    w_copies[0].wait()
    w_copies[1].wait()

    def g_arrived(k, _):
        arrived(rg.at[slot_rows(k)], S_G + k)
        return 0

    lax.fori_loop(1, 32, g_arrived, 0)

    def upward_tile(i, _):
        rows = pl.ds(pl.multiple_of(i * 256, 256), 256)
        upw[:, rows] = dot_nt(rg[...], wout[rows, :])
        return 0

    lax.fori_loop(0, HID // 256, upward_tile, 0)

    for chunk in (0, 3, 1, 2):
        rows = slice(chunk * 128, chunk * 128 + 128)

        def x_arrived(k, _):
            arrived(rx.at[slot_rows(k)], S_X + k)
            return 0

        lax.fori_loop(max(chunk * 8, 1), chunk * 8 + 8, x_arrived, 0)

        def hidden_tile(i, gate):
            cols = pl.ds(pl.multiple_of(i * 256, 256), 256)
            pre = dot(rx[rows, :], win[:, cols])
            upward = upw[rows, cols]
            sig = jax.nn.sigmoid(pre)
            unit = pre * sig * upward
            hg[:, cols] = (upward * sig * (1.0 + pre * (1.0 - sig))).astype(BF16)
            return gate + unit[:, 0:128] + unit[:, 128:256]

        gate = lax.fori_loop(0, HID // 256, hidden_tile, jnp.zeros((FR, 128), F32))
        gate_row = jnp.sum(jnp.transpose(gate), axis=0, keepdims=True).astype(BF16).astype(F32)
        gs[chunk] = gate_row

        def grad_tile(i, _):
            cols = pl.ds(pl.multiple_of(i * 256, 256), 256)
            rs[rows, cols] = dot_nt(hg[...], win[cols, :]).astype(BF16)
            return 0

        lax.fori_loop(0, D // 256, grad_tile, 0)

        def give_back(k, _):
            dz, dj = div(k, 4), rem(k, 4)
            there = rem(8 - dz, 8) * 4 + dj
            device = near(dz, dj)
            remote(rs.at[slot_rows(k)], rr.at[slot_rows(there)], S_R + k, S_R + there, device).start()
            remote(gs.at[chunk], gr.at[there], S_T + k, S_T + there, device).start()
            return 0

        lax.fori_loop(max(chunk * 8, 1), chunk * 8 + 8, give_back, 0)
    rr[0:CAP, :] = rs[0:CAP, :]
    gr[0] = gs[0]

    qr[0] = qs[head_rows(z), :]
    kva[0:FR, :] = ks[z]

    def to_planes(dz, _):
        h = rem(z + dz, 8)
        back = 8 - dz
        device = near(dz, 0)
        remote(qs.at[head_rows(h)], qr.at[back], S_Q + dz, S_Q + back, device).start()
        remote(
            ks.at[h], kva.at[pl.ds(pl.multiple_of(back * FR, FR), FR)], S_KV + dz, S_KV + back, device
        ).start()
        return 0

    lax.fori_loop(1, 8, to_planes, 0)

    def r_arrived(k, _):
        arrived(rr.at[slot_rows(k)], S_R + k)
        return 0

    lax.fori_loop(1, 32, r_arrived, 0)
    gates = gates_ref[...]
    for n in range(4):
        cols = slice(n * 256, n * 256 + 256)
        back = rr[:, cols]
        grad = up_ref[:, cols].astype(F32)
        grad = grad + gates[:, 0:1] * dot(pick[0], back)
        grad = grad + gates[:, 1:2] * dot(pick[1], back)
        gm[:, cols] = grad.astype(BF16)

    halo_g_out = [
        remote(gm.at[pl.ds(FR - 16, 16)], halo_g.at[0], S_HG, S_HG, along(1)),
        remote(gm.at[pl.ds(0, 16)], halo_g.at[1], S_HG + 1, S_HG + 1, along(-1)),
    ]
    for copy in halo_g_out:
        copy.start()
    gwide[16 : 16 + FR, :] = gm[...].astype(F32)

    def kv_arrived(k, _):
        arrived(kva.at[pl.ds(pl.multiple_of(k * FR, FR), FR)], S_KV + k)
        return 0

    lax.fori_loop(1, 8, kv_arrived, 0)
    for dj in (2, 3, 1):
        remote(
            kva.at[pl.ds(0, 1024)], kva.at[pl.ds(dj * 1024, 1024)], S_KVP + dj, S_KVP + dj, near(0, dj, True)
        ).start()

    def tap_tile(i, _):
        cols = lane_tile(i)
        here = gwide[pl.ds(16, FR), cols]
        for o in range(1, TAPS + 1):
            part = jnp.sum((wide[pl.ds(o, FR), cols] * here).reshape(16, 8, 128), axis=0)
            dc_s[i, pl.ds(o - 1, 1), :] = jnp.sum(part, axis=0, keepdims=True)
        dc_s[i, pl.ds(TAPS, 1), :] = jnp.zeros((1, 128), F32)
        return 0

    lax.fori_loop(0, 8, tap_tile, 0)

    def taps_out(dz, _):
        remote(dc_s.at[rem(z + dz, 8)], dc_r.at[8 - dz], S_DC1 + dz, S_DC1 + 8 - dz, near(dz, 0)).start()
        return 0

    for side in range(2):
        arrived(halo_g.at[side], S_HG + side)
    gwide[0:16, :] = halo_g[0].astype(F32) * not_first
    gwide[16 + FR : 32 + FR, :] = halo_g[1].astype(F32) * not_last
    convolve(gwide, dmid_ref, True)

    w_copies[2].wait()
    grad_out = dot_nt(oproj[...], dmid_ref[...]).astype(BF16)
    delta = jnp.sum((grad_out.astype(F32) * attn_t[...]).reshape(HEADS, 64, FR), axis=1)
    for h in range(HEADS):
        dos[h * 80 : h * 80 + 64, :] = grad_out[h * 64 : h * 64 + 64, :]
        dos[h * 80 + 64 : h * 80 + 80, :] = three_rows(delta, h)
    dor[0] = dos[head_rows(z), :]

    def dout_to_planes(dz, _):
        back = 8 - dz
        remote(dos.at[head_rows(rem(z + dz, 8))], dor.at[back], S_DO + dz, S_DO + back, near(dz, 0)).start()
        return 0

    lax.fori_loop(1, 8, dout_to_planes, 0)
    lax.fori_loop(1, 8, taps_out, 0)

    def q_arrived(k, _):
        arrived(qr.at[k], S_Q + k)
        return 0

    lax.fori_loop(1, 8, q_arrived, 0)
    qz[64:128, :] = jnp.zeros((64, 1024), BF16)
    for b in range(8):
        cols = slice(b * 128, b * 128 + 128)
        qz[0:64, cols] = qr[b, 0:64, :]
        nrow[:, cols] = jnp.sum(qr[b, 64:80, :].astype(F32), axis=0, keepdims=True)
        qn[cols, :] = jnp.transpose(qz[:, cols].astype(F32)).astype(BF16)
    for dj in (1, 2, 3):
        arrived(kva.at[pl.ds(dj * 1024, 1024)], S_KVP + dj)

    def prob_tile(i, _):
        rows = pl.ds(pl.multiple_of(i * 256, 256), 256)
        tile = kva[rows, :]
        kt[:, rows] = jnp.transpose(tile.astype(F32))[0:64, :].astype(BF16)
        pt[rows, :] = jnp.exp(dot(tile, qz[...]) - nrow[...]).astype(BF16)
        return 0

    lax.fori_loop(0, KEYS // 256, prob_tile, 0)

    def do_arrived(k, _):
        arrived(dor.at[k], S_DO + k)
        return 0

    lax.fori_loop(1, 8, do_arrived, 0)
    doz[0:64, :] = jnp.zeros((64, 1024), BF16)
    for b in range(8):
        cols = slice(b * 128, b * 128 + 128)
        doz[64:128, cols] = dor[b, 0:64, :]
        drow[:, cols] = jnp.sum(dor[b, 64:80, :].astype(F32), axis=0, keepdims=True)
        don[cols, :] = jnp.transpose(doz[:, cols].astype(F32)).astype(BF16)
    dqa[...] = jnp.zeros((64, 1024), F32)

    for dj in (3, 2, 1, 0):

        def score_tile(i, _):
            at = pl.multiple_of(i * 256, 256)
            rows = pl.ds(pl.multiple_of(dj * 1024 + at, 256), 256)
            prob = pt[rows, :]
            dprob = dot(kva[rows, :], doz[...]) - drow[...]
            score = (prob.astype(F32) * dprob).astype(BF16)
            both_grads = dot(score, qn[...]) + dot(prob, don[...])
            if dj:
                dkv_s[dj - 1, pl.ds(at, 256), :] = both_grads.astype(BF16)
            else:
                dkv0[pl.ds(at, 256), :] = both_grads
            dqa[...] += dot(kt[:, rows], score)
            return 0

        lax.fori_loop(0, 4, score_tile, 0)
        if dj:
            remote(
                dkv_s.at[dj - 1], dkv_r.at[dj - 1], S_DKVP + dj, S_DKVP + dj, near(0, dj, True)
            ).start()

    for b in range(8):
        dq_s[b] = (dqa[:, b * 128 : b * 128 + 128] * 0.125).astype(BF16)
    z_rows = pl.ds(pl.multiple_of(z * 64, 64), 64)
    dq_o[z_rows, :] = dq_s[0]

    def dq_home(dz, _):
        remote(dq_s.at[dz], dq_o.at[z_rows], S_DQ + dz, S_DQ + 8 - dz, near(dz, 0)).start()
        return 0

    lax.fori_loop(1, 8, dq_home, 0)

    def dc1_arrived(k, _):
        arrived(dc_r.at[k], S_DC1 + k)
        return 0

    lax.fori_loop(1, 8, dc1_arrived, 0)
    taps = dc_s[z]
    for b in range(1, 8):
        taps = taps + dc_r[b]
    dc1[...] = taps
    dc2[j] = taps
    for dj in (2, 3, 1):
        remote(dc1, dc2.at[j], S_DC2 + dj, S_DC2 + dj, near(0, dj, True)).start()

    for dj in (3, 2, 1):
        arrived(dkv_r.at[dj - 1], S_DKVP + dj)

    def sum_keys(k, _):
        n = rem(k + 1, 8)
        rows = pl.ds(pl.multiple_of(n * FR, FR), FR)
        total = dkv0[rows, :]
        for p in range(3):
            total = total + dkv_r[p, rows, :].astype(F32)
        dkv_z[n] = total.astype(BF16)

        @pl.when(n > 0)
        def _():
            remote(dkv_z.at[n], dkv_o.at[z], S_DKVZ + n, S_DKVZ + rem(8 - n, 8), near(n, 0)).start()

        return 0

    lax.fori_loop(0, 8, sum_keys, 0)
    dkv_o[z] = dkv_z[0]

    for dj in (1, 2, 3):
        arrived(dc1, S_DC2 + dj)
    dc3[...] = (dc2[0] + dc2[1]) + (dc2[2] + dc2[3])
    dcf[z] = dc3[...]

    def taps_home(dz, _):
        remote(dc3, dcf.at[z], S_DC3 + dz, S_DC3 + 8 - dz, near(dz, 0)).start()
        return 0

    lax.fori_loop(1, 8, taps_home, 0)

    def t_arrived(k, _):
        arrived(gr.at[k], S_T + k)
        return 0

    lax.fori_loop(1, 32, t_arrived, 0)
    for k in range(EXPERTS):
        g2[k : k + 1, :] = gr[k]
    spot_lane = lax.broadcasted_iota(jnp.int32, (FR, EXPERTS), 1)
    lane_128 = lax.broadcasted_iota(jnp.int32, (FR, 128), 1)
    units = g2[...].astype(BF16)
    for r in range(2):
        of_spot = jnp.where(spot_lane == spot[:, r : r + 1], 1.0, 0.0).astype(BF16)
        line = dot(of_spot, units)
        own = lane_128 == (sid[:, r : r + 1] & 127)
        dgates_ref[:, r : r + 1] = jnp.sum(jnp.where(own, line, 0.0), axis=1, keepdims=True).astype(BF16)

    def dq_arrived(k, _):
        arrived(dq_s.at[k], S_DQ + k)
        return 0

    lax.fori_loop(1, 8, dq_arrived, 0)
    for n in range(4):
        cols = slice(n * 128, n * 128 + 128)
        dq_ref[:, cols] = jnp.transpose(dq_o[cols, :].astype(F32)).astype(BF16)

    def dkv_arrived(k, _):
        arrived(dkv_z.at[k], S_DKVZ + k)
        return 0

    lax.fori_loop(1, 8, dkv_arrived, 0)
    for n in range(4):
        cols = slice(n * 128, n * 128 + 128)
        first = lanes_below((FR, 128), 64)
        one, two = dkv_o[2 * n].astype(F32), dkv_o[2 * n + 1].astype(F32)
        dk_ref[:, cols] = jnp.where(first, one, pltpu.roll(two, 64, 1)).astype(BF16)
        dv_ref[:, cols] = jnp.where(first, pltpu.roll(one, 64, 1), two).astype(BF16)

    def dc3_arrived(k, _):
        arrived(dc3, S_DC3 + k)
        return 0

    lax.fori_loop(1, 8, dc3_arrived, 0)
    for n in range(8):
        dconv_ref[:, n * 128 : n * 128 + 128] = dcf[n, 0:TAPS, :]

    def rows_left(k, _):
        for first in (S_G, S_X, S_R):
            sent(sg.at[slot_rows(k)], first + k)
        sent(gr.at[k], S_T + k)
        return 0

    lax.fori_loop(1, 32, rows_left, 0)

    def blocks_left(k, _):
        sent(qr.at[k], S_Q + k)
        sent(ks.at[k], S_KV + k)
        sent(dor.at[k], S_DO + k)
        sent(dkv_z.at[k], S_DKVZ + k)
        sent(dq_s.at[k], S_DQ + k)
        sent(dc_r.at[k], S_DC1 + k)
        sent(dc3, S_DC3 + k)
        return 0

    lax.fori_loop(1, 8, blocks_left, 0)
    for copy in halo_m_out + halo_g_out:
        copy.wait_send()
    for dj in (1, 2, 3):
        sent(kva.at[pl.ds(0, 1024)], S_KVP + dj)
        sent(dkv_s.at[dj - 1], S_DKVP + dj)
        sent(dc1, S_DC2 + dj)


def on_device(*args):
    vmem, anywhere = pl.BlockSpec(memory_space=pltpu.VMEM), pl.BlockSpec(memory_space=pl.ANY)
    in_specs = [vmem] * 14
    for n in (7, 12, 13):
        in_specs[n] = anywhere
    V = pltpu.VMEM
    scratch = [
        V((D, HID), BF16), V((HID, D), BF16), V((512, D), BF16),
        V((160, D), F32), V((160, D), F32), V((32, D), F32),
        V((2, 16, D), BF16), V((2, 16, D), BF16), V((FR, D), BF16), V((2, FR, ROWS), BF16),
        V((ROWS, D), BF16), V((ROWS, D), BF16), V((ROWS, D), BF16), V((ROWS, D), BF16),
        V((ROWS, HID), F32), V((FR, HID), BF16), V((ROWS, D), BF16), V((ROWS, D), BF16),
        V((4, 1, 128), F32), V((EXPERTS, 1, 128), F32), V((EXPERTS, 128), F32),
        V((640, 128), BF16), V((8, 80, 128), BF16), V((8, FR, 128), BF16), V((KEYS, 128), BF16),
        V((128, 1024), BF16), V((1024, 128), BF16), V((1, 1024), F32), V((64, KEYS), BF16), V((KEYS, 1024), BF16),
        V((640, 128), BF16), V((8, 80, 128), BF16), V((128, 1024), BF16), V((1024, 128), BF16), V((1, 1024), F32),
        V((512, FR), F32), V((3, 1024, 128), BF16), V((3, 1024, 128), BF16),
        V((1024, 128), F32), V((8, FR, 128), BF16), V((8, FR, 128), BF16),
        V((64, 1024), F32), V((8, 64, 128), BF16), V((512, 128), BF16),
        V((8, 32, 128), F32), V((8, 32, 128), F32), V((32, 128), F32), V((4, 32, 128), F32), V((32, 128), F32),
        V((8, 32, 128), F32), V((FR, 128), F32),
        pltpu.SemaphoreType.DMA((SEMS,)), pltpu.SemaphoreType.DMA((SEMS,)), pltpu.SemaphoreType.DMA((3,)),
    ]
    shape = jax.ShapeDtypeStruct
    return pl.pallas_call(
        kernel,
        out_shape=(
            shape((FR, D), BF16), shape((FR, 512), BF16), shape((FR, 512), BF16), shape((FR, 512), BF16),
            shape((TAPS, D), F32), shape((FR, 2), BF16),
        ),
        in_specs=in_specs,
        out_specs=(vmem,) * 6,
        scratch_shapes=scratch,
        compiler_params=pltpu.CompilerParams(
            collective_id=0, has_side_effects=True, vmem_limit_bytes=58 * 1024 * 1024
        ),
        name="conformer_backward",
    )(*args)


def solution(mesh):
    frames = P(("grp", "ctx"), None)
    in_specs = (frames,) * 7 + (P(), P()) + (frames,) * 3 + (P("ctx", None, None),) * 2
    out_specs = (frames,) * 4 + (P("grp", None), frames)
    return jax.shard_map(on_device, mesh=mesh, in_specs=in_specs, out_specs=out_specs, check_vma=False)
```

time: 723 us -> 159 us (0.22)
  waiting for transfers between devices: 259 us -> 0 us
  starting transfers between devices: 143 us -> 0 us
  Pallas kernels: 0 us -> 142 us
  blocking collectives: 133 us -> 0 us
  matrix products: 110 us -> 0 us
  local copies, waits for them, and re-layouts: 56.9 us -> 14.9 us
  other arithmetic: 14 us -> 0 us
    ppermute x132 -> x0, waiting for transfers between devices: 191 us -> none  [the longest x128 191 us: from_behind(): return lax.ppermute(value, axis, pairs)]
    pallas_call x0 -> x1, Pallas kernels: none -> 142 us  [on_device(): pl.pallas_call(kernel, out_shape=(shape((FR, D), BF16), shape((FR, 512),...]
    psum x1 -> x0, blocking collectives: 133 us -> none  [on_device(): lax.psum(local_terms.astype(jnp.bfloat16), 'ctx').astype(jnp.float32)]
    dot_general x164 -> x0, matrix products: 110 us -> none  [the longest x32 28 us: key_terms(): jnp.einsum('hqk,qhd->khd', softmax_low, dout_rows, preferred_element_type...]
    ppermute x132 -> x0, starting transfers between devices: 108 us -> none  [the longest x128 103 us: from_behind(): return lax.ppermute(value, axis, pairs)]
    all_to_all x4 -> x0, waiting for transfers between devices: 68.2 us -> none  [the longest x1 26.3 us: on_device(): lax.all_to_all(send_rows, 'ctx', split_axis=0, concat_axis=0, tiled=True)]
    all_to_all x4 -> x0, starting transfers between devices: 34.9 us -> none  [the longest x1 15.5 us: on_device(): lax.all_to_all(send_rows, 'ctx', split_axis=0, concat_axis=0, tiled=True)]
    while x64 -> x0, local copies, waits for them, and re-layouts: 29.3 us -> none
  transfers between devices with their start and end apart: 136 -> 0, of which waited for: 68 -> 0; matrix products, arithmetic and copies ran while one was open for 21% -> 0% of each run, Pallas kernels for 0% -> 0%
where the time goes in v1:
time: 159 us; the launch traced here: 158 us
  Pallas kernels  142 us (89%)
  local copies, waits for them, and re-layouts  14.9 us (9%)
    pallas_call x1, Pallas kernels, on_device(): pl.pallas_call(kernel, out_shape=(shape((FR, D), BF16), shape((FR, 512),...  142 us
    unnamed x9, local copies, waits for them, and re-layouts  13.6 us

profile of v1, /device:TPU:6, one launch (start us, length us, event | category | flops | bytes accessed | tf_op | source)
XLA Modules:
  0.0 157.7 jit_solution(16660053743486089783)
XLA Ops:
  0.6 1.4 copy.20.norm_ref
  2.0 1.4 copy.21.gates_ref
  3.5 1.4 copy.22.ids_ref
  4.9 1.4 copy.23.slots_ref
  6.3 142.1 %conformer_backward.1 = (bf16[128,1024]{1,0:T(8,128)(2,1)}, bf16[128,512]{1,0:T(8,128)(2,1)}, bf16[128,512]{1,0:T(8,128)(2,1)}, bf16[128,512]{1,0:T(8,128)(2,1)}...) custom-call(bf16[128,1024]{1,0:T(8,128)(2,1)} %mid_ref.1, bf16[128,1024]{1,0:T(8,128)(2,1)} %up_ref.1, ...), custom_call_target="tpu_custom_call" | custom-call | tf_op jit(solution)/shard_map/conformer_backward/pallas_call | solution.py:570
  148.4 1.4 copy.24
  149.7 1.7 %copy.30 = bf16[128,1024]{1,0:T(8,128)(2,1)} copy(bf16[128,1024]{1,0:T(8,128)(2,1)} %get-tuple-element.18) | data formatting | bytes 524288
  151.4 1.6 copy.31
  153.0 1.6 copy.32
  154.5 1.6 copy.33
  156.1 1.6 copy.34

commit v2 on v1

--- a/solution.py
+++ b/solution.py
@@ -37,6 +37,11 @@
     return lax.dot_general(a, b, NT, preferred_element_type=F32)
 
 
+def loop(name, first, last, body, init=0):
+    with jax.named_scope(name):
+        return lax.fori_loop(first, last, body, init)
+
+
 def rem(a, b):
     return lax.rem(a, jnp.int32(b))
 
@@ -61,13 +66,15 @@
 
 
 def kernel(
-    mid_ref, up_ref, q_ref, k_ref, v_ref, attn_ref, norm_ref, oproj_hbm, cw_ref, gates_ref, ids_ref,
-    slots_ref, win_hbm, wout_hbm,
+    mid_hbm, up_hbm, q_hbm, k_hbm, v_hbm, attn_hbm, norm_hbm, oproj_hbm, cw_hbm, gates_hbm, ids_hbm,
+    slots_hbm, win_hbm, wout_hbm,
+    dmid_hbm, dq_hbm, dk_hbm, dv_hbm, dconv_hbm, dgates_hbm,
+    mid_ref, up_ref, q_ref, k_ref, v_ref, attn_ref, norm_ref, cw_ref, gates_ref, ids_ref, slots_ref,
     dmid_ref, dq_ref, dk_ref, dv_ref, dconv_ref, dgates_ref,
     win, wout, oproj, wide, gwide, cwf, halo_m, halo_g, gm, pick, sg, sx, rg, rx, upw, hg, rs, rr,
-    gs, gr, g2, qs, qr, ks, kva, qz, qn, nrow, kt, pt, dos, dor, doz, don, drow, attn_t, dkv_s, dkv_r,
-    dkv0, dkv_z, dkv_o, dqa, dq_s, dq_o, dc_s, dc_r, dc1, dc2, dc3, dcf, tmp,
-    ssem, rsem, wsem,
+    gs, gr, qs, qr, ks, kva, qz, qn, nrow, kt, pt, dos, dor, doz, don, drow, attn_t, dkv_s, dkv_r,
+    dkv0, dkv_z, dkv_o, dqa, dq_s, dq_o, dc_s, dc_r, dc1, dc2, dc3, dcf, tmp, columns,
+    dkv2, ssem, rsem, wsem, isem, osem,
 ):
     grp, ctx = lax.axis_index("grp"), lax.axis_index("ctx")
     ylo, xx = div(grp, 4), rem(grp, 4)
@@ -111,6 +118,26 @@
         pltpu.make_async_copy(win_hbm.at[0], win, wsem.at[1]),
         pltpu.make_async_copy(oproj_hbm, oproj, wsem.at[2]),
     ]
+    inputs = dict(
+        ids=(ids_hbm, ids_ref), slots=(slots_hbm, slots_ref), up=(up_hbm, up_ref), mid=(mid_hbm, mid_ref),
+        cw=(cw_hbm, cw_ref), gates=(gates_hbm, gates_ref), norm=(norm_hbm, norm_ref), q=(q_hbm, q_ref),
+        attn=(attn_hbm, attn_ref), k=(k_hbm, k_ref), v=(v_hbm, v_ref),
+    )
+    loads = {name: pltpu.make_async_copy(*pair, isem.at[n]) for n, (name, pair) in enumerate(inputs.items())}
+    stores = [
+        pltpu.make_async_copy(here, there, osem.at[n])
+        for n, (here, there) in enumerate((
+            (dmid_ref, dmid_hbm), (dq_ref, dq_hbm), (dk_ref, dk_hbm), (dv_ref, dv_hbm), (dconv_ref, dconv_hbm),
+            (dgates_ref, dgates_hbm),
+        ))
+    ]
+    for copy in loads.values():
+        copy.start()
+
+    def loaded(*names):
+        for name in names:
+            loads[name].wait()
+
     barrier = pltpu.get_barrier_semaphore()
 
     def greet(k, _):
@@ -118,7 +145,7 @@
         pl.semaphore_signal(barrier, inc=1, device_id=near(dz, dj), device_id_type=MESH)
         return 0
 
-    lax.fori_loop(1, 32, greet, 0)
+    loop("greet", 1, 32, greet)
     for dj in (2, 3):
         pl.semaphore_signal(barrier, inc=1, device_id=near(0, dj, True), device_id_type=MESH)
     for step in (1, -1):
@@ -126,18 +153,14 @@
     for copy in w_copies:
         copy.start()
 
+    loaded("ids", "slots", "up")
     ids, slot = ids_ref[...], slots_ref[...]
     planes_on = (jnp.right_shift(ids, 2) - z + 8) & 7
     in_plane = ((jnp.right_shift(ids, 1) + yhi) & 1) * 2 + ((ids + core) & 1)
     spot = planes_on * 4 + in_plane
     sid = spot * CAP + slot
-    lane = lax.broadcasted_iota(jnp.int32, (FR, ROWS), 1)
-    both = jnp.zeros((FR, ROWS), F32)
-    for r in range(2):
-        hit = jnp.where(lane == sid[:, r : r + 1], 1.0, 0.0).astype(F32)
-        pick[r] = hit.astype(BF16)
-        both = both + hit
-    spread = jnp.transpose(both).astype(BF16)
+    at = lax.broadcasted_iota(jnp.int32, (ROWS, FR), 0)
+    spread = jnp.where((at == sid[0:1, :]) | (at == sid[1:2, :]), 1.0, 0.0).astype(BF16)
 
     for n in range(4):
         rows = slice(n * 128, n * 128 + 128)
@@ -146,6 +169,7 @@
 
     pl.semaphore_wait(barrier, 35)
 
+    loaded("mid")
     halo_m_out = [
         remote(mid_ref.at[pl.ds(FR - 16, 16)], halo_m.at[0], S_HM, S_HM, along(1)),
         remote(mid_ref.at[pl.ds(0, 16)], halo_m.at[1], S_HM + 1, S_HM + 1, along(-1)),
@@ -163,14 +187,20 @@
             ).start()
             return 0
 
-        lax.fori_loop(1, 32, body, 0)
+        loop("body", 1, 32, body)
 
     spread_out(sg, rg, S_G)
 
+    loaded("cw", "gates", "norm", "q", "attn", "k", "v")
     cwf[0:TAPS, :] = cw_ref[...].astype(F32)
+    norm_t = norm_ref[...]
     tmp[...] = jnp.zeros((FR, 128), F32)
-    tmp[:, 0:HEADS] = norm_ref[...]
-    norm_t = jnp.transpose(tmp[...])
+    tmp[0:2, :] = sid.astype(F32)
+    tmp[2:4, :] = gates_ref[...]
+    columns[...] = jnp.transpose(tmp[...])
+    lane = lax.broadcasted_iota(jnp.int32, (FR, ROWS), 1)
+    for r in range(2):
+        pick[r] = jnp.where(lane == columns[:, r : r + 1].astype(jnp.int32), 1.0, 0.0).astype(BF16)
     for n in range(4):
         cols = slice(n * 128, n * 128 + 128)
         q_t = jnp.transpose(q_ref[:, cols].astype(F32) * 0.125).astype(BF16)
@@ -199,7 +229,7 @@
         return pl.ds(pl.multiple_of(i * 128, 128), 128)
 
     def convolve(src, dst, backward):
-        def body(i, _):
+        def conv_tile(i, _):
             cols = lane_tile(i)
             total = src[pl.ds(16, FR), cols]
             for o in range(1, TAPS + 1):
@@ -208,7 +238,7 @@
             dst[:, cols] = total.astype(BF16)
             return 0
 
-        lax.fori_loop(0, 8, body, 0)
+        loop("conv_tile", 0, 8, conv_tile)
 
     convolve(wide, gm, False)
     for n in range(4):
@@ -224,14 +254,14 @@
         arrived(rg.at[slot_rows(k)], S_G + k)
         return 0
 
-    lax.fori_loop(1, 32, g_arrived, 0)
+    loop("g_arrived", 1, 32, g_arrived)
 
     def upward_tile(i, _):
         rows = pl.ds(pl.multiple_of(i * 256, 256), 256)
         upw[:, rows] = dot_nt(rg[...], wout[rows, :])
         return 0
 
-    lax.fori_loop(0, HID // 256, upward_tile, 0)
+    loop("upward_tile", 0, HID // 256, upward_tile)
 
     for chunk in (0, 3, 1, 2):
         rows = slice(chunk * 128, chunk * 128 + 128)
@@ -240,7 +270,7 @@
             arrived(rx.at[slot_rows(k)], S_X + k)
             return 0
 
-        lax.fori_loop(max(chunk * 8, 1), chunk * 8 + 8, x_arrived, 0)
+        loop("x_arrived", max(chunk * 8, 1), chunk * 8 + 8, x_arrived)
 
         def hidden_tile(i, gate):
             cols = pl.ds(pl.multiple_of(i * 256, 256), 256)
@@ -251,7 +281,7 @@
             hg[:, cols] = (upward * sig * (1.0 + pre * (1.0 - sig))).astype(BF16)
             return gate + unit[:, 0:128] + unit[:, 128:256]
 
-        gate = lax.fori_loop(0, HID // 256, hidden_tile, jnp.zeros((FR, 128), F32))
+        gate = loop("hidden_tile", 0, HID // 256, hidden_tile, jnp.zeros((FR, 128), F32))
         gate_row = jnp.sum(jnp.transpose(gate), axis=0, keepdims=True).astype(BF16).astype(F32)
         gs[chunk] = gate_row
 
@@ -260,7 +290,7 @@
             rs[rows, cols] = dot_nt(hg[...], win[cols, :]).astype(BF16)
             return 0
 
-        lax.fori_loop(0, D // 256, grad_tile, 0)
+        loop("grad_tile", 0, D // 256, grad_tile)
 
         def give_back(k, _):
             dz, dj = div(k, 4), rem(k, 4)
@@ -270,37 +300,38 @@
             remote(gs.at[chunk], gr.at[there], S_T + k, S_T + there, device).start()
             return 0
 
-        lax.fori_loop(max(chunk * 8, 1), chunk * 8 + 8, give_back, 0)
+        loop("give_back", max(chunk * 8, 1), chunk * 8 + 8, give_back)
     rr[0:CAP, :] = rs[0:CAP, :]
     gr[0] = gs[0]
 
     qr[0] = qs[head_rows(z), :]
     kva[0:FR, :] = ks[z]
 
-    def to_planes(dz, _):
-        h = rem(z + dz, 8)
+    def keys_to_planes(dz, _):
         back = 8 - dz
-        device = near(dz, 0)
-        remote(qs.at[head_rows(h)], qr.at[back], S_Q + dz, S_Q + back, device).start()
-        remote(
-            ks.at[h], kva.at[pl.ds(pl.multiple_of(back * FR, FR), FR)], S_KV + dz, S_KV + back, device
-        ).start()
-        return 0
-
-    lax.fori_loop(1, 8, to_planes, 0)
+        rows = pl.ds(pl.multiple_of(back * FR, FR), FR)
+        remote(ks.at[rem(z + dz, 8)], kva.at[rows], S_KV + dz, S_KV + back, near(dz, 0)).start()
+        return 0
+
+    def queries_to_planes(dz, _):
+        back = 8 - dz
+        remote(qs.at[head_rows(rem(z + dz, 8))], qr.at[back], S_Q + dz, S_Q + back, near(dz, 0)).start()
+        return 0
+
+    loop("keys_to_planes", 1, 8, keys_to_planes)
+    loop("queries_to_planes", 1, 8, queries_to_planes)
 
     def r_arrived(k, _):
         arrived(rr.at[slot_rows(k)], S_R + k)
         return 0
 
-    lax.fori_loop(1, 32, r_arrived, 0)
-    gates = gates_ref[...]
+    loop("r_arrived", 1, 32, r_arrived)
     for n in range(4):
         cols = slice(n * 256, n * 256 + 256)
         back = rr[:, cols]
         grad = up_ref[:, cols].astype(F32)
-        grad = grad + gates[:, 0:1] * dot(pick[0], back)
-        grad = grad + gates[:, 1:2] * dot(pick[1], back)
+        grad = grad + columns[:, 2:3] * dot(pick[0], back)
+        grad = grad + columns[:, 3:4] * dot(pick[1], back)
         gm[:, cols] = grad.astype(BF16)
 
     halo_g_out = [
@@ -315,11 +346,10 @@
         arrived(kva.at[pl.ds(pl.multiple_of(k * FR, FR), FR)], S_KV + k)
         return 0
 
-    lax.fori_loop(1, 8, kv_arrived, 0)
-    for dj in (2, 3, 1):
-        remote(
-            kva.at[pl.ds(0, 1024)], kva.at[pl.ds(dj * 1024, 1024)], S_KVP + dj, S_KVP + dj, near(0, dj, True)
-        ).start()
+    loop("kv_arrived", 1, 8, kv_arrived)
+    own_keys = kva.at[pl.ds(0, 1024)]
+    for dj in (2, 1):
+        remote(own_keys, kva.at[pl.ds(dj * 1024, 1024)], S_KVP + dj, S_KVP + dj, near(0, dj, True)).start()
 
     def tap_tile(i, _):
         cols = lane_tile(i)
@@ -330,7 +360,7 @@
         dc_s[i, pl.ds(TAPS, 1), :] = jnp.zeros((1, 128), F32)
         return 0
 
-    lax.fori_loop(0, 8, tap_tile, 0)
+    loop("tap_tile", 0, 8, tap_tile)
 
     def taps_out(dz, _):
         remote(dc_s.at[rem(z + dz, 8)], dc_r.at[8 - dz], S_DC1 + dz, S_DC1 + 8 - dz, near(dz, 0)).start()
@@ -341,6 +371,7 @@
     gwide[0:16, :] = halo_g[0].astype(F32) * not_first
     gwide[16 + FR : 32 + FR, :] = halo_g[1].astype(F32) * not_last
     convolve(gwide, dmid_ref, True)
+    stores[0].start()
 
     w_copies[2].wait()
     grad_out = dot_nt(oproj[...], dmid_ref[...]).astype(BF16)
@@ -355,37 +386,42 @@
         remote(dos.at[head_rows(rem(z + dz, 8))], dor.at[back], S_DO + dz, S_DO + back, near(dz, 0)).start()
         return 0
 
-    lax.fori_loop(1, 8, dout_to_planes, 0)
-    lax.fori_loop(1, 8, taps_out, 0)
+    loop("dout_to_planes", 1, 8, dout_to_planes)
+    loop("taps_out", 1, 8, taps_out)
 
     def q_arrived(k, _):
         arrived(qr.at[k], S_Q + k)
         return 0
 
-    lax.fori_loop(1, 8, q_arrived, 0)
+    loop("q_arrived", 1, 8, q_arrived)
     qz[64:128, :] = jnp.zeros((64, 1024), BF16)
     for b in range(8):
         cols = slice(b * 128, b * 128 + 128)
         qz[0:64, cols] = qr[b, 0:64, :]
         nrow[:, cols] = jnp.sum(qr[b, 64:80, :].astype(F32), axis=0, keepdims=True)
         qn[cols, :] = jnp.transpose(qz[:, cols].astype(F32)).astype(BF16)
-    for dj in (1, 2, 3):
-        arrived(kva.at[pl.ds(dj * 1024, 1024)], S_KVP + dj)
-
-    def prob_tile(i, _):
-        rows = pl.ds(pl.multiple_of(i * 256, 256), 256)
-        tile = kva[rows, :]
-        kt[:, rows] = jnp.transpose(tile.astype(F32))[0:64, :].astype(BF16)
-        pt[rows, :] = jnp.exp(dot(tile, qz[...]) - nrow[...]).astype(BF16)
-        return 0
-
-    lax.fori_loop(0, KEYS // 256, prob_tile, 0)
+    for dj in range(4):
+        if dj:
+            arrived(kva.at[pl.ds(dj * 1024, 1024)], S_KVP + dj)
+        if dj == 2:
+            remote(
+                kva.at[pl.ds(2048, 1024)], kva.at[pl.ds(3072, 1024)], S_KVP + 3, S_KVP + 3, near(0, 1)
+            ).start()
+
+        def prob_tile(i, _):
+            rows = pl.ds(pl.multiple_of(i * 256, 256), 256)
+            tile = kva[rows, :]
+            kt[:, rows] = jnp.transpose(tile.astype(F32))[0:64, :].astype(BF16)
+            pt[rows, :] = jnp.exp(dot(tile, qz[...]) - nrow[...]).astype(BF16)
+            return 0
+
+        loop("prob_tile", dj * 4, dj * 4 + 4, prob_tile)
 
     def do_arrived(k, _):
         arrived(dor.at[k], S_DO + k)
         return 0
 
-    lax.fori_loop(1, 8, do_arrived, 0)
+    loop("do_arrived", 1, 8, do_arrived)
     doz[0:64, :] = jnp.zeros((64, 1024), BF16)
     for b in range(8):
         cols = slice(b * 128, b * 128 + 128)
@@ -403,18 +439,26 @@
             dprob = dot(kva[rows, :], doz[...]) - drow[...]
             score = (prob.astype(F32) * dprob).astype(BF16)
             both_grads = dot(score, qn[...]) + dot(prob, don[...])
-            if dj:
+            if dj % 2:
                 dkv_s[dj - 1, pl.ds(at, 256), :] = both_grads.astype(BF16)
             else:
-                dkv0[pl.ds(at, 256), :] = both_grads
+                (dkv2 if dj else dkv0)[pl.ds(at, 256), :] = both_grads
             dqa[...] += dot(kt[:, rows], score)
             return 0
 
-        lax.fori_loop(0, 4, score_tile, 0)
+        loop("score_tile", 0, 4, score_tile)
+        if dj == 2:
+            arrived(dkv_r.at[2], S_DKVP + 3)
+
+            def join_tile(i, _):
+                rows = pl.ds(pl.multiple_of(i * 256, 256), 256)
+                dkv_s[1, rows, :] = (dkv2[rows, :] + dkv_r[2, rows, :].astype(F32)).astype(BF16)
+                return 0
+
+            loop("join_tile", 0, 4, join_tile)
         if dj:
-            remote(
-                dkv_s.at[dj - 1], dkv_r.at[dj - 1], S_DKVP + dj, S_DKVP + dj, near(0, dj, True)
-            ).start()
+            device = near(0, 2, True) if dj == 2 else near(0, 1)
+            remote(dkv_s.at[dj - 1], dkv_r.at[dj - 1], S_DKVP + dj, S_DKVP + dj, device).start()
 
     for b in range(8):
         dq_s[b] = (dqa[:, b * 128 : b * 128 + 128] * 0.125).astype(BF16)
@@ -425,13 +469,13 @@
         remote(dq_s.at[dz], dq_o.at[z_rows], S_DQ + dz, S_DQ + 8 - dz, near(dz, 0)).start()
         return 0
 
-    lax.fori_loop(1, 8, dq_home, 0)
+    loop("dq_home", 1, 8, dq_home)
 
     def dc1_arrived(k, _):
         arrived(dc_r.at[k], S_DC1 + k)
         return 0
 
-    lax.fori_loop(1, 8, dc1_arrived, 0)
+    loop("dc1_arrived", 1, 8, dc1_arrived)
     taps = dc_s[z]
     for b in range(1, 8):
         taps = taps + dc_r[b]
@@ -440,14 +484,14 @@
     for dj in (2, 3, 1):
         remote(dc1, dc2.at[j], S_DC2 + dj, S_DC2 + dj, near(0, dj, True)).start()
 
-    for dj in (3, 2, 1):
+    for dj in (1, 2):
         arrived(dkv_r.at[dj - 1], S_DKVP + dj)
 
     def sum_keys(k, _):
         n = rem(k + 1, 8)
         rows = pl.ds(pl.multiple_of(n * FR, FR), FR)
         total = dkv0[rows, :]
-        for p in range(3):
+        for p in range(2):
             total = total + dkv_r[p, rows, :].astype(F32)
         dkv_z[n] = total.astype(BF16)
 
@@ -457,7 +501,7 @@
 
         return 0
 
-    lax.fori_loop(0, 8, sum_keys, 0)
+    loop("sum_keys", 0, 8, sum_keys)
     dkv_o[z] = dkv_z[0]
 
     for dj in (1, 2, 3):
@@ -469,52 +513,56 @@
         remote(dc3, dcf.at[z], S_DC3 + dz, S_DC3 + 8 - dz, near(dz, 0)).start()
         return 0
 
-    lax.fori_loop(1, 8, taps_home, 0)
+    loop("taps_home", 1, 8, taps_home)
 
     def t_arrived(k, _):
         arrived(gr.at[k], S_T + k)
         return 0
 
-    lax.fori_loop(1, 32, t_arrived, 0)
+    loop("t_arrived", 1, 32, t_arrived)
+    tmp[...] = jnp.zeros((FR, 128), F32)
     for k in range(EXPERTS):
-        g2[k : k + 1, :] = gr[k]
-    spot_lane = lax.broadcasted_iota(jnp.int32, (FR, EXPERTS), 1)
-    lane_128 = lax.broadcasted_iota(jnp.int32, (FR, 128), 1)
-    units = g2[...].astype(BF16)
+        tmp[k : k + 1, :] = gr[k]
+    units = jnp.transpose(tmp[...]).astype(BF16)
+    at = lax.broadcasted_iota(jnp.int32, (128, FR), 0)
     for r in range(2):
-        of_spot = jnp.where(spot_lane == spot[:, r : r + 1], 1.0, 0.0).astype(BF16)
-        line = dot(of_spot, units)
-        own = lane_128 == (sid[:, r : r + 1] & 127)
-        dgates_ref[:, r : r + 1] = jnp.sum(jnp.where(own, line, 0.0), axis=1, keepdims=True).astype(BF16)
+        line = dot(units, jnp.where(at == spot[r : r + 1, :], 1.0, 0.0).astype(BF16))
+        own = at == (sid[r : r + 1, :] & 127)
+        dgates_ref[r : r + 1, :] = jnp.sum(jnp.where(own, line, 0.0), axis=0, keepdims=True).astype(BF16)
+    stores[5].start()
 
     def dq_arrived(k, _):
         arrived(dq_s.at[k], S_DQ + k)
         return 0
 
-    lax.fori_loop(1, 8, dq_arrived, 0)
+    loop("dq_arrived", 1, 8, dq_arrived)
     for n in range(4):
         cols = slice(n * 128, n * 128 + 128)
         dq_ref[:, cols] = jnp.transpose(dq_o[cols, :].astype(F32)).astype(BF16)
+    stores[1].start()
 
     def dkv_arrived(k, _):
         arrived(dkv_z.at[k], S_DKVZ + k)
         return 0
 
-    lax.fori_loop(1, 8, dkv_arrived, 0)
+    loop("dkv_arrived", 1, 8, dkv_arrived)
     for n in range(4):
         cols = slice(n * 128, n * 128 + 128)
         first = lanes_below((FR, 128), 64)
         one, two = dkv_o[2 * n].astype(F32), dkv_o[2 * n + 1].astype(F32)
         dk_ref[:, cols] = jnp.where(first, one, pltpu.roll(two, 64, 1)).astype(BF16)
         dv_ref[:, cols] = jnp.where(first, pltpu.roll(one, 64, 1), two).astype(BF16)
+    stores[2].start()
+    stores[3].start()
 
     def dc3_arrived(k, _):
         arrived(dc3, S_DC3 + k)
         return 0
 
-    lax.fori_loop(1, 8, dc3_arrived, 0)
+    loop("dc3_arrived", 1, 8, dc3_arrived)
     for n in range(8):
         dconv_ref[:, n * 128 : n * 128 + 128] = dcf[n, 0:TAPS, :]
+    stores[4].start()
 
     def rows_left(k, _):
         for first in (S_G, S_X, S_R):
@@ -522,7 +570,7 @@
         sent(gr.at[k], S_T + k)
         return 0
 
-    lax.fori_loop(1, 32, rows_left, 0)
+    loop("rows_left", 1, 32, rows_left)
 
     def blocks_left(k, _):
         sent(qr.at[k], S_Q + k)
@@ -534,28 +582,46 @@
         sent(dc3, S_DC3 + k)
         return 0
 
-    lax.fori_loop(1, 8, blocks_left, 0)
+    loop("blocks_left", 1, 8, blocks_left)
     for copy in halo_m_out + halo_g_out:
         copy.wait_send()
     for dj in (1, 2, 3):
         sent(kva.at[pl.ds(0, 1024)], S_KVP + dj)
         sent(dkv_s.at[dj - 1], S_DKVP + dj)
         sent(dc1, S_DC2 + dj)
+    for copy in stores:
+        copy.wait()
+
+
+def store(*refs):
+    held, sems = refs[12:18], refs[18]
+    ins = [pltpu.make_async_copy(refs[n], held[n], sems.at[n]) for n in range(6)]
+    outs = [pltpu.make_async_copy(held[n], refs[6 + n], sems.at[6 + n]) for n in range(6)]
+    for copy in ins:
+        copy.start()
+    for first, second in zip(ins, outs):
+        first.wait()
+        second.start()
+    for copy in outs:
+        copy.wait()
 
 
 def on_device(*args):
-    vmem, anywhere = pl.BlockSpec(memory_space=pltpu.VMEM), pl.BlockSpec(memory_space=pl.ANY)
-    in_specs = [vmem] * 14
-    for n in (7, 12, 13):
-        in_specs[n] = anywhere
+    args = list(args)
+    for n in (6, 9, 10, 11):
+        args[n] = args[n].T
+    anywhere = pl.BlockSpec(memory_space=pl.ANY)
     V = pltpu.VMEM
     scratch = [
+        V((FR, D), BF16), V((FR, D), BF16), V((FR, 512), BF16), V((FR, 512), BF16), V((FR, 512), BF16), V((FR, 512), BF16),
+        V((HEADS, FR), F32), V((TAPS, D), BF16), V((2, FR), F32), V((2, FR), jnp.int32), V((2, FR), jnp.int32),
+        V((FR, D), BF16), V((FR, 512), BF16), V((FR, 512), BF16), V((FR, 512), BF16), V((TAPS, D), F32), V((2, FR), BF16),
         V((D, HID), BF16), V((HID, D), BF16), V((512, D), BF16),
         V((160, D), F32), V((160, D), F32), V((32, D), F32),
         V((2, 16, D), BF16), V((2, 16, D), BF16), V((FR, D), BF16), V((2, FR, ROWS), BF16),
         V((ROWS, D), BF16), V((ROWS, D), BF16), V((ROWS, D), BF16), V((ROWS, D), BF16),
         V((ROWS, HID), F32), V((FR, HID), BF16), V((ROWS, D), BF16), V((ROWS, D), BF16),
-        V((4, 1, 128), F32), V((EXPERTS, 1, 128), F32), V((EXPERTS, 128), F32),
+        V((4, 1, 128), F32), V((EXPERTS, 1, 128), F32),
         V((640, 128), BF16), V((8, 80, 128), BF16), V((8, FR, 128), BF16), V((KEYS, 128), BF16),
         V((128, 1024), BF16), V((1024, 128), BF16), V((1, 1024), F32), V((64, KEYS), BF16), V((KEYS, 1024), BF16),
         V((640, 128), BF16), V((8, 80, 128), BF16), V((128, 1024), BF16), V((1024, 128), BF16), V((1, 1024), F32),
@@ -563,24 +629,37 @@
         V((1024, 128), F32), V((8, FR, 128), BF16), V((8, FR, 128), BF16),
         V((64, 1024), F32), V((8, 64, 128), BF16), V((512, 128), BF16),
         V((8, 32, 128), F32), V((8, 32, 128), F32), V((32, 128), F32), V((4, 32, 128), F32), V((32, 128), F32),
-        V((8, 32, 128), F32), V((FR, 128), F32),
+        V((8, 32, 128), F32), V((FR, 128), F32), V((FR, 128), F32),
+        V((1024, 128), F32),
         pltpu.SemaphoreType.DMA((SEMS,)), pltpu.SemaphoreType.DMA((SEMS,)), pltpu.SemaphoreType.DMA((3,)),
+        pltpu.SemaphoreType.DMA((11,)), pltpu.SemaphoreType.DMA((6,)),
     ]
     shape = jax.ShapeDtypeStruct
-    return pl.pallas_call(
+    out_shape = (
+        shape((FR, D), BF16), shape((FR, 512), BF16), shape((FR, 512), BF16), shape((FR, 512), BF16),
+        shape((TAPS, D), F32), shape((2, FR), BF16),
+    )
+    found = pl.pallas_call(
         kernel,
-        out_shape=(
-            shape((FR, D), BF16), shape((FR, 512), BF16), shape((FR, 512), BF16), shape((FR, 512), BF16),
-            shape((TAPS, D), F32), shape((FR, 2), BF16),
-        ),
-        in_specs=in_specs,
-        out_specs=(vmem,) * 6,
+        out_shape=out_shape,
+        in_specs=[anywhere] * 14,
+        out_specs=(anywhere,) * 6,
         scratch_shapes=scratch,
         compiler_params=pltpu.CompilerParams(
             collective_id=0, has_side_effects=True, vmem_limit_bytes=58 * 1024 * 1024
         ),
         name="conformer_backward",
     )(*args)
+    results = pl.pallas_call(
+        store,
+        out_shape=out_shape,
+        in_specs=[anywhere] * 6,
+        out_specs=(anywhere,) * 6,
+        scratch_shapes=[V(o.shape, o.dtype) for o in out_shape] + [pltpu.SemaphoreType.DMA((12,))],
+        compiler_params=pltpu.CompilerParams(vmem_limit_bytes=60 * 1024 * 1024),
+        name="store",
+    )(*found)
+    return (*results[:5], results[5].T)
 
 
 def solution(mesh):

time: 159 us -> 134 us (0.84)
  local copies, waits for them, and re-layouts: 14.9 us -> 0 us
  Pallas kernels: 142 us -> 133 us
    unnamed x9 -> x0, local copies, waits for them, and re-layouts: 13.6 us -> none
    pallas_call x1 -> x2, Pallas kernels: 142 us -> 133 us  [the longest x1 131 us: on_device(): pl.pallas_call(kernel, out_shape=out_shape, in_specs=[anywhere] * 14, out...]
where the time goes in v2:
time: 134 us; the launch traced here: 133 us
  Pallas kernels  133 us (99%)
    pallas_call x1, Pallas kernels, on_device(): pl.pallas_call(kernel, out_shape=out_shape, in_specs=[anywhere] * 14, out...  131 us

profile of v2, /device:TPU:6, one launch (start us, length us, event | category | flops | bytes accessed | tf_op | source)
XLA Modules:
  0.0 133.3 jit_solution(5383446012108890087)
XLA Ops:
  0.6 130.7 %conformer_backward.1 = (bf16[128,1024]{1,0:T(8,128)(2,1)}, bf16[128,512]{1,0:T(8,128)(2,1)}, bf16[128,512]{1,0:T(8,128)(2,1)}, bf16[128,512]{1,0:T(8,128)(2,1)}...) custom-call(bf16[128,1024]{1,0:T(8,128)(2,1)} %mid_hbm.1, bf16[128,1024]{1,0:T(8,128)(2,1)} %up_hbm.1, ...), custom_call_target="tpu_custom_call" | custom-call | tf_op jit(solution)/shard_map/conformer_backward/pallas_call | solution.py:642
  131.4 1.9 %store.1 = (bf16[128,1024]{1,0:T(8,128)(2,1)}, bf16[128,512]{1,0:T(8,128)(2,1)}, bf16[128,512]{1,0:T(8,128)(2,1)}, bf16[128,512]{1,0:T(8,128)(2,1)}, f32[31,1024]{1,0:T(8,128)}, /*index=5*/bf16[2,128]{1,0:T(2,128)(2,1)}) custom-call(bf16[128,1024]{1,0:T(8,128)(2,1)} %get-tuple-element.18.refs_0_, bf16[128,512]{1,0:T(8,128)(2,1)} %get-tuple-element.19.refs_1_, ...), custom_call_target="tpu_custom_call" | custom-call | tf_op jit(solution)/shard_map/store/pallas_call | solution.py:653

commit v3 on v2

--- a/solution.py
+++ b/solution.py
@@ -24,7 +24,8 @@
 S_Q, S_KV, S_KVP = 132, 140, 148
 S_DO, S_DKVP, S_DKVZ, S_DQ = 152, 160, 164, 172
 S_DC1, S_DC2, S_DC3 = 180, 188, 192
-SEMS = 200
+S_DKVP2 = 200
+SEMS = 204
 
 NT = (((1,), (1,)), ((), ()))
 
@@ -417,6 +418,19 @@
 
         loop("prob_tile", dj * 4, dj * 4 + 4, prob_tile)
 
+    def dc1_arrived(k, _):
+        arrived(dc_r.at[k], S_DC1 + k)
+        return 0
+
+    loop("dc1_arrived", 1, 8, dc1_arrived)
+    taps = dc_s[z]
+    for b in range(1, 8):
+        taps = taps + dc_r[b]
+    dc1[...] = taps
+    dc2[j] = taps
+    for dj in (2, 3, 1):
+        remote(dc1, dc2.at[j], S_DC2 + dj, S_DC2 + dj, near(0, dj, True)).start()
+
     def do_arrived(k, _):
         arrived(dor.at[k], S_DO + k)
         return 0
@@ -430,35 +444,66 @@
         don[cols, :] = jnp.transpose(doz[:, cols].astype(F32)).astype(BF16)
     dqa[...] = jnp.zeros((64, 1024), F32)
 
-    for dj in (3, 2, 1, 0):
-
-        def score_tile(i, _):
-            at = pl.multiple_of(i * 256, 256)
-            rows = pl.ds(pl.multiple_of(dj * 1024 + at, 256), 256)
-            prob = pt[rows, :]
-            dprob = dot(kva[rows, :], doz[...]) - drow[...]
-            score = (prob.astype(F32) * dprob).astype(BF16)
-            both_grads = dot(score, qn[...]) + dot(prob, don[...])
-            if dj % 2:
-                dkv_s[dj - 1, pl.ds(at, 256), :] = both_grads.astype(BF16)
-            else:
-                (dkv2 if dj else dkv0)[pl.ds(at, 256), :] = both_grads
-            dqa[...] += dot(kt[:, rows], score)
-            return 0
-
-        loop("score_tile", 0, 4, score_tile)
-        if dj == 2:
-            arrived(dkv_r.at[2], S_DKVP + 3)
-
-            def join_tile(i, _):
-                rows = pl.ds(pl.multiple_of(i * 256, 256), 256)
-                dkv_s[1, rows, :] = (dkv2[rows, :] + dkv_r[2, rows, :].astype(F32)).astype(BF16)
+    def sum_blocks(half):
+        first = S_DKVP2 if half else S_DKVP
+        part = pl.ds(half * 512, 512)
+        for dj in (1, 2):
+            arrived(dkv_r.at[dj - 1, part], first + dj)
+        for m, n in enumerate(((2, 3, 4, 5), (0, 1, 6, 7))[half]):
+            rows = slice(half * 512 + m * FR, half * 512 + m * FR + FR)
+            total = dkv0[rows, :] + dkv_r[0, rows, :].astype(F32) + dkv_r[1, rows, :].astype(F32)
+            dkv_z[n] = total.astype(BF16)
+            if n:
+                remote(dkv_z.at[n], dkv_o.at[z], S_DKVZ + n, S_DKVZ + 8 - n, near(n, 0)).start()
+
+    for half in range(2):
+        first = S_DKVP2 if half else S_DKVP
+        part = pl.ds(half * 512, 512)
+        for dj in (3, 2, 1, 0):
+
+            def score_tile(i, _):
+                tile_at = i * 3 if half else i + 1
+                rows = pl.ds(pl.multiple_of(dj * 1024 + tile_at * 256, 256), 256)
+                kept = pl.ds(pl.multiple_of(half * 512 + i * 256, 256), 256)
+                prob = pt[rows, :]
+                dprob = dot(kva[rows, :], doz[...]) - drow[...]
+                score = (prob.astype(F32) * dprob).astype(BF16)
+                both_grads = dot(score, qn[...]) + dot(prob, don[...])
+                if dj % 2:
+                    dkv_s[dj - 1, kept, :] = both_grads.astype(BF16)
+                else:
+                    (dkv2 if dj else dkv0)[kept, :] = both_grads
+                dqa[...] += dot(kt[:, rows], score)
                 return 0
 
-            loop("join_tile", 0, 4, join_tile)
-        if dj:
-            device = near(0, 2, True) if dj == 2 else near(0, 1)
-            remote(dkv_s.at[dj - 1], dkv_r.at[dj - 1], S_DKVP + dj, S_DKVP + dj, device).start()
+            loop("score_tile", 0, 2, score_tile)
+            if dj == 2:
+                arrived(dkv_r.at[2, part], first + 3)
+
+                def join_tile(i, _):
+                    rows = pl.ds(pl.multiple_of(half * 512 + i * 256, 256), 256)
+                    dkv_s[1, rows, :] = (dkv2[rows, :] + dkv_r[2, rows, :].astype(F32)).astype(BF16)
+                    return 0
+
+                loop("join_tile", 0, 2, join_tile)
+            if dj:
+                device = near(0, 2, True) if dj == 2 else near(0, 1)
+                remote(
+                    dkv_s.at[dj - 1, part], dkv_r.at[dj - 1, part], first + dj, first + dj, device
+                ).start()
+            if half == 0 and dj == 3:
+                for place_at in (1, 2, 3):
+                    arrived(dc1, S_DC2 + place_at)
+                dc3[...] = (dc2[0] + dc2[1]) + (dc2[2] + dc2[3])
+                dcf[z] = dc3[...]
+
+                def taps_home(dz, _):
+                    remote(dc3, dcf.at[z], S_DC3 + dz, S_DC3 + 8 - dz, near(dz, 0)).start()
+                    return 0
+
+                loop("taps_home", 1, 8, taps_home)
+            if half == 1 and dj == 2:
+                sum_blocks(0)
 
     for b in range(8):
         dq_s[b] = (dqa[:, b * 128 : b * 128 + 128] * 0.125).astype(BF16)
@@ -471,49 +516,8 @@
 
     loop("dq_home", 1, 8, dq_home)
 
-    def dc1_arrived(k, _):
-        arrived(dc_r.at[k], S_DC1 + k)
-        return 0
-
-    loop("dc1_arrived", 1, 8, dc1_arrived)
-    taps = dc_s[z]
-    for b in range(1, 8):
-        taps = taps + dc_r[b]
-    dc1[...] = taps
-    dc2[j] = taps
-    for dj in (2, 3, 1):
-        remote(dc1, dc2.at[j], S_DC2 + dj, S_DC2 + dj, near(0, dj, True)).start()
-
-    for dj in (1, 2):
-        arrived(dkv_r.at[dj - 1], S_DKVP + dj)
-
-    def sum_keys(k, _):
-        n = rem(k + 1, 8)
-        rows = pl.ds(pl.multiple_of(n * FR, FR), FR)
-        total = dkv0[rows, :]
-        for p in range(2):
-            total = total + dkv_r[p, rows, :].astype(F32)
-        dkv_z[n] = total.astype(BF16)
-
-        @pl.when(n > 0)
-        def _():
-            remote(dkv_z.at[n], dkv_o.at[z], S_DKVZ + n, S_DKVZ + rem(8 - n, 8), near(n, 0)).start()
-
-        return 0
-
-    loop("sum_keys", 0, 8, sum_keys)
+    sum_blocks(1)
     dkv_o[z] = dkv_z[0]
-
-    for dj in (1, 2, 3):
-        arrived(dc1, S_DC2 + dj)
-    dc3[...] = (dc2[0] + dc2[1]) + (dc2[2] + dc2[3])
-    dcf[z] = dc3[...]
-
-    def taps_home(dz, _):
-        remote(dc3, dcf.at[z], S_DC3 + dz, S_DC3 + 8 - dz, near(dz, 0)).start()
-        return 0
-
-    loop("taps_home", 1, 8, taps_home)
 
     def t_arrived(k, _):
         arrived(gr.at[k], S_T + k)
@@ -587,7 +591,8 @@
         copy.wait_send()
     for dj in (1, 2, 3):
         sent(kva.at[pl.ds(0, 1024)], S_KVP + dj)
-        sent(dkv_s.at[dj - 1], S_DKVP + dj)
+        sent(dkv_s.at[dj - 1, pl.ds(0, 512)], S_DKVP + dj)
+        sent(dkv_s.at[dj - 1, pl.ds(0, 512)], S_DKVP2 + dj)
         sent(dc1, S_DC2 + dj)
     for copy in stores:
         copy.wait()

time: 134 us -> 134 us (level); the launches traced: 133 us -> 132 us
  Pallas kernels: 133 us -> 131 us
    pallas_call x1, Pallas kernels: 131 us -> 129 us  [on_device(): pl.pallas_call(kernel, out_shape=out_shape, in_specs=[anywhere] * 14, out...]
where the time goes in v3:
time: 134 us; the launch traced here: 132 us
  Pallas kernels  131 us (98%)
    pallas_call x1, Pallas kernels, on_device(): pl.pallas_call(kernel, out_shape=out_shape, in_specs=[anywhere] * 14, out...  129 us

profile of v3, /device:TPU:6, one launch (start us, length us, event | category | flops | bytes accessed | tf_op | source)
XLA Modules:
  0.0 131.6 jit_solution(17668512395607952985)
XLA Ops:
  0.6 129.1 %conformer_backward.1 = (bf16[128,1024]{1,0:T(8,128)(2,1)}, bf16[128,512]{1,0:T(8,128)(2,1)}, bf16[128,512]{1,0:T(8,128)(2,1)}, bf16[128,512]{1,0:T(8,128)(2,1)}...) custom-call(bf16[128,1024]{1,0:T(8,128)(2,1)} %mid_hbm.1, bf16[128,1024]{1,0:T(8,128)(2,1)} %up_hbm.1, ...), custom_call_target="tpu_custom_call" | custom-call | tf_op jit(solution)/shard_map/conformer_backward/pallas_call | solution.py:647
  129.7 1.9 %store.1 = (bf16[128,1024]{1,0:T(8,128)(2,1)}, bf16[128,512]{1,0:T(8,128)(2,1)}, bf16[128,512]{1,0:T(8,128)(2,1)}, bf16[128,512]{1,0:T(8,128)(2,1)}, f32[31,1024]{1,0:T(8,128)}, /*index=5*/bf16[2,128]{1,0:T(2,128)(2,1)}) custom-call(bf16[128,1024]{1,0:T(8,128)(2,1)} %get-tuple-element.18.refs_0_, bf16[128,512]{1,0:T(8,128)(2,1)} %get-tuple-element.19.refs_1_, ...), custom_call_target="tpu_custom_call" | custom-call | tf_op jit(solution)/shard_map/store/pallas_call | solution.py:658
